TPU v7x, 512 devices: a whole 4x8x8 slice. The times are simulated.
512 devices in a mesh: expert: 32 (over x, z), head: 16 (over y, core).
Axes of the slice: x: 4, y: 8, z: 8, core: 2. Of those that a mesh axis runs over, the one named last changes fastest.
Arguments:
- queries: bfloat16 [32, 128, 576], P('expert', 'head'), may hold values from -136 to 136
- kv_cache: bfloat16 [32, 12288, 576], P('expert', 'head'), may hold values from -4 to 4
- block_ids: int32 [32, 32], P('expert'), may hold values from 0 to 191, as said below
- w_uv: bfloat16 [128, 512, 128], P('head'), may hold values from -0.25 to 0.25
- o_proj: bfloat16 [16384, 3584], P('head', 'expert'), may hold values from -0.046875 to 0.046875
- residual: bfloat16 [32, 3584], P(None, 'expert'), may hold values from -6 to 6
- moe_gain: bfloat16 [3584], P('expert'), may hold values from 0.099609375 to 1.8984375
- w_gate: bfloat16 [32, 3584, 2048], P('expert', None, 'head'), may hold values from -0.09375 to 0.09375
- w_up: bfloat16 [32, 3584, 2048], P('expert', None, 'head'), may hold values from -0.09375 to 0.09375
- w_down: bfloat16 [32, 2048, 3584], P('expert', 'head'), may hold values from -0.125 to 0.125
- expert_ids: int32 [32, 8], replicated, may hold values from 0 to 31, all different within a row; in each aligned block of 32 rows (0 to 31, 32 to 63, ...) at most 16 rows name the same one
- gate_weights: float32 [32, 8], replicated, may hold values from 0.05 to 0.3
Outputs:
- layer_output: bfloat16 [32, 3584], P('head', 'expert')
Inputs may be any that keep to these rules, and one draw needn't show every extreme that they name: `block_ids`: each row names 32 different blocks. `expert_ids`: each row names 8 different experts; no expert is named by more than 16 of the 32 rows, a bound that some block reaches.
All inputs are finite; a program needn't handle non-finite values.
Results may differ from a plain program's by a relative error of at most 0.0075.
Values may be sent and summed in bfloat16 or wider, within the bound.
No kernel may reach another device: no remote copies, remote signals or barrier semaphores. Data moves between devices by JAX's collectives and lax.ppermute only.
A program may use at most 64 MiB of HBM per device.

v0:
```python
import jax
import jax.numpy as jnp
from jax import lax
from jax.sharding import PartitionSpec as P

D = 3584
LAT = 512
BLK = 64


score_scale = 192 ** (-0.5)
norm_eps = 1e-06


def slot_tables(expert_ids, gate_weights, experts, capacity):
    onehot = expert_ids[:, :, None] == jnp.arange(experts, dtype=jnp.int32)[None, None, :]
    picked = jnp.sum(onehot.astype(jnp.int32), axis=1)
    weight = jnp.sum(
        jnp.where(onehot, gate_weights[:, :, None], jnp.zeros_like(gate_weights[:, :, None])),
        axis=1,
    )
    before = jnp.cumsum(picked, axis=0) - picked
    matched = (picked[:, :, None] == 1) & (
        before[:, :, None] == jnp.arange(capacity, dtype=jnp.int32)[None, None, :]
    )
    dispatch_map = matched.astype(gate_weights.dtype)
    combine_map = dispatch_map * weight[:, :, None]
    row_count = expert_ids.shape[0]
    return (
        dispatch_map.reshape(row_count, experts * capacity),
        combine_map.reshape(row_count, experts * capacity),
    )


def chosen_tokens(block_ids, count):
    blocks_of = jnp.arange(count, dtype=jnp.int32) // BLK
    return jnp.any(block_ids[:, :, None] == blocks_of[None, None, :], axis=1)


def masked_scores(query_vals, cache_vals, selected):
    scores = (
        jnp.einsum("rhd,rtd->rht", query_vals, cache_vals, preferred_element_type=jnp.float32)
        * score_scale
    )
    return jnp.where(selected[:, None, :], scores, -1e30)


def weighted(scores, highest, selected, cache_vals):
    exponent = jnp.where(selected[:, None, :], jnp.exp(scores - highest[:, :, None]), 0.0)
    denominator = jnp.sum(exponent, axis=2)
    latent = jnp.einsum(
        "rht,rtc->rhc",
        exponent.astype(jnp.bfloat16),
        cache_vals[:, :, :LAT],
        preferred_element_type=jnp.float32,
    )
    return (latent, denominator)


def local(
    queries,
    kv_cache,
    block_ids,
    w_uv,
    o_proj,
    residual,
    moe_gain,
    w_gate,
    w_up,
    w_down,
    expert_ids,
    gate_weights,
):
    gathered = lax.all_gather(kv_cache, "head", axis=1, tiled=True)
    selected = chosen_tokens(block_ids, gathered.shape[1])
    scores = masked_scores(queries, gathered, selected)
    highest = jnp.max(scores, axis=2)
    latent, denominator = weighted(scores, highest, selected, gathered)
    attended = (latent / denominator[:, :, None]).astype(jnp.bfloat16)
    head_vals = jnp.einsum(
        "rhc,hcv->rhv", attended, w_uv, preferred_element_type=jnp.float32
    ).astype(jnp.bfloat16)
    head_flat = head_vals.reshape(head_vals.shape[0], -1)
    attn_part = jnp.dot(
        lax.all_gather(head_flat, "expert", axis=0, tiled=True),
        o_proj,
        preferred_element_type=jnp.float32,
    )
    row_count = expert_ids.shape[0]
    row_share = row_count // lax.axis_size("head")
    first_row = lax.axis_index("head") * row_share
    gain_wide = moe_gain.astype(jnp.float32)[None, :]
    attn = lax.psum(attn_part, "head")
    mixed_state = (residual.astype(jnp.float32) + attn).astype(jnp.bfloat16)
    widened = mixed_state.astype(jnp.float32)
    squares = lax.psum(jnp.sum(widened * widened, axis=1), "expert")
    normed = (widened * lax.rsqrt(squares / D + norm_eps)[:, None] * gain_wide).astype(jnp.bfloat16)
    kept_rows = lax.dynamic_slice_in_dim(mixed_state, first_row, row_share, 0)
    experts = lax.axis_size("expert") * w_gate.shape[0]
    capacity = min(2 * (row_count // lax.axis_size("expert")) * expert_ids.shape[1], row_count)
    dispatch_map, combine_map = slot_tables(expert_ids, gate_weights, experts, capacity)
    send_rows = jnp.einsum(
        "rs,rd->sd", dispatch_map.astype(jnp.bfloat16), normed, preferred_element_type=jnp.float32
    )
    send_rows = send_rows.astype(jnp.bfloat16).reshape(experts, capacity, normed.shape[1])
    tokens = lax.all_to_all(send_rows, "expert", split_axis=0, concat_axis=2, tiled=True)[0]
    gate_act = jnp.dot(tokens, w_gate[0], preferred_element_type=jnp.float32)
    up_act = jnp.dot(tokens, w_up[0], preferred_element_type=jnp.float32)
    hidden = (jax.nn.silu(gate_act) * up_act).astype(jnp.bfloat16)
    partial_out = jnp.dot(hidden, w_down[0], preferred_element_type=jnp.float32)[None]
    returned = lax.all_to_all(partial_out, "expert", split_axis=2, concat_axis=0, tiled=True)
    moe_part = jnp.dot(
        combine_map,
        returned.reshape(experts * capacity, -1),
        precision=lax.Precision.HIGHEST,
        preferred_element_type=jnp.float32,
    )
    moe_out = lax.psum_scatter(moe_part, "head", scatter_dimension=0, tiled=True)
    return (kept_rows.astype(jnp.float32) + moe_out).astype(jnp.bfloat16)


def solution(mesh):
    in_specs = (
        P("expert", "head", None),
        P("expert", "head", None),
        P("expert", None),
        P("head", None, None),
        P("head", "expert"),
        P(None, "expert"),
        P("expert"),
        P("expert", None, "head"),
        P("expert", None, "head"),
        P("expert", "head", None),
        P(),
        P(),
    )
    out_specs = P("head", "expert")
    return jax.shard_map(local, mesh=mesh, in_specs=in_specs, out_specs=out_specs, check_vma=False)
```

profile of v0, /device:TPU:1, one launch (start us, length us, event | category | flops | bytes accessed | tf_op | source)
XLA Modules:
  0.0 383.3 jit_solution(12115137074266013993)
XLA Ops:
  6.5 0.0 all-gather.3.cloned.1.call-start
  6.5 0.7 all-gather.3.cloned.1.call-update
  7.3 0.8 copy.30
  8.0 0.1 convert_reduce_fusion
  8.1 0.1 reduce_window_sum.11
  8.2 0.1 copy.32
  8.3 0.1 copy.31
  8.4 0.1 eq.90
  8.5 0.7 convert_element_type.59
  9.1 0.1 convert_convert_fusion
  9.3 0.9 compare_reduce_fusion
  10.2 0.0 copy-start.3
  10.2 0.0 copy-start.4
  10.3 90.6 %all-gather.3.cloned.1.call-done = bf16[1,12288,576]{1,2,0:T(8,128)(2,1)} async-done(((bf16[1,768,576]{1,2,0:T(8,128)(2,1)}), bf16[1,12288,576]{1,2,0:T(8,128)(2,1)}) %all-gather.3.cloned.1.call-update) | async-done | bytes 14155792 | tf_op jit(solution)/shard_map/all_gather | solution.py:74
  100.8 6.3 %fusion.52 = (f32[8]{0:T(128)S(1)}, f32[8,12288]{1,0:T(8,128)S(1)}) fusion(bf16[1,12288,576]{1,2,0:T(8,128)(2,1)} %all-gather.3.cloned.1.call-done, bf16[1,8,576]{2,1,0:T(8,128)(2,1)} %param.12, pred[12288]{0:T(1024)(128)(4,1)S(1)} %compare_reduce_fusion), kind=kOutput, calls=%fused_computation.66 | convolution fusion | flops 113541112 | bytes 14570528 | tf_op jit(solution)/shard_map/rhd,rtd->rht/dot_general | solution.py:42
  107.2 0.3 fusion.19
  107.5 2.4 copy-done.1
  109.9 3.3 fusion.13
  113.2 0.0 copy-done
  113.2 0.3 fusion.37
  113.5 34.7 %all-gather = bf16[32,1,1024]{2,1,0:T(2,128)(2,1)S(1)} all-gather(bf16[1,1,1024]{2,1,0:T(2,128)(2,1)S(1)} %reshape.189), channel_id=1, replica_groups=mesh['expert'=32,'head'=16] {'expert'}, dimensions={0}, use_global_device_ids=true | all-gather | bytes 67584 | tf_op jit(solution)/shard_map/all_gather | solution.py:85
  148.2 0.0 copy-done.3
  148.2 0.2 fusion.28
  148.4 52.3 %psum.14 = f32[32,112]{1,0:T(8,128)S(1)} all-reduce(f32[32,112]{1,0:T(8,128)S(1)} %fusion.28), channel_id=1, replica_groups=mesh['expert'=32,'head'=16] {'head'}, use_global_device_ids=true, to_apply=%region_3.4 | all-reduce | flops 3584 | bytes 28672 | tf_op jit(solution)/shard_map/psum | solution.py:93
  200.7 0.1 fusion.34
  200.8 58.4 %psum.15 = f32[32]{0:T(128)S(1)} all-reduce(f32[32]{0:T(128)S(1)} %get-tuple-element.5), channel_id=1, replica_groups=mesh['expert'=32,'head'=16] {'expert'}, use_global_device_ids=true, to_apply=%region_8.9 | all-reduce | flops 32 | bytes 256 | tf_op jit(solution)/shard_map/psum | solution.py:96
  259.3 0.3 convolution_convert_fusion
  259.6 0.1 copy.35
  259.7 12.1 %all_to_all.30 = bf16[32,16,112]{2,1,0:T(8,128)(2,1)S(1)} all-to-all(bf16[32,16,112]{2,1,0:T(8,128)(2,1)S(1)} %bitcast.76), channel_id=1, replica_groups=mesh['expert'=32,'head'=16] {'expert'}, dimensions={0} | all-to-all | bytes 229376 | tf_op jit(solution)/shard_map/all_to_all | solution.py:106
  271.8 0.2 squeeze.12
  272.0 0.2 fusion.17
  272.3 2.1 fusion.10
  274.4 0.5 broadcast.159
  274.9 17.1 %reduce.5 = f32[3584,16]{1,0:T(8,128)} reduce(f32[3584,1,16]{2,1,0:T(1,128)S(1)} %bitcast.72, f32[]{:T(128)} %broadcast.159), dimensions={1}, to_apply=%bitcast.59.reduce_sub_computation | reduce | bytes 458756
  292.0 2.8 reshape.195
  294.8 4.0 %all-to-all-start.1 = ((f32[32,1,1792]{2,1,0:T(1,128)}), f32[32,1,1792]{2,1,0:T(1,128)S(1)}, u32[]{:S(2)}, u32[]{:S(2)}) async-start(f32[32,1,1792]{2,1,0:T(1,128)} %reshape.195), calls=%async_computation.1 | async-start | bytes 458752 | tf_op jit(solution)/shard_map/all_to_all | solution.py:111
  298.9 0.1 copy.33
  299.0 0.1 select_reduce_fusion
  299.1 0.1 copy.34
  299.2 1.3 dynamic-slice
  301.3 0.1 fusion.22
  301.3 7.1 %all-to-all-done.1 = f32[32,1,1792]{2,1,0:T(1,128)S(1)} async-done(((f32[32,1,1792]{2,1,0:T(1,128)}), f32[32,1,1792]{2,1,0:T(1,128)S(1)}, u32[]{:S(2)}, u32[]{:S(2)}) %all-to-all-start.1) | async-done | bytes 229408 | tf_op jit(solution)/shard_map/all_to_all | solution.py:111
  308.4 1.2 reduce.6
  309.6 3.4 reshape.196
  313.0 0.5 copy.38
  313.5 0.6 fusion.53
  314.1 61.9 %all-reduce = f32[32,112]{1,0:T(8,128)S(1)} all-reduce(f32[32,112]{1,0:T(8,128)S(1)} %fusion.53), channel_id=2, replica_groups=mesh['expert'=32,'head'=16] {'head'}, use_global_device_ids=true, to_apply=%region_9.10.clone | all-reduce | flops 3584 | bytes 28672
  376.0 0.5 fusion.49
  (15 shorter events, 0.1 us)
Async XLA Ops:
  6.5 106.7 %copy-start = (bf16[8,512,128]{2,1,0:T(8,128)(2,1)S(1)}, bf16[8,512,128]{2,1,0:T(8,128)(2,1)}, u32[]{:S(2)}) copy-start(bf16[8,512,128]{2,1,0:T(8,128)(2,1)} %param.15) | copy-start | bytes 3145732
  6.5 94.3 %all-gather.3.cloned.1.call-start = ((), (), s32[]{:S(2)}) async-start(), calls=%async_computation.2 | async-start | bytes 15040512 | tf_op jit(solution)/shard_map/all_gather | solution.py:74
  10.2 138.0 %copy-start.3 = (bf16[1024,112]{0,1:T(8,128)(2,1)S(1)}, bf16[1024,112]{0,1:T(8,128)(2,1)}, u32[]{:S(2)}) copy-start(bf16[1024,112]{0,1:T(8,128)(2,1)} %param.16) | copy-start | bytes 688132
  10.2 190.5 %copy-start.4 = (bf16[32,112]{1,0:T(8,128)(2,1)S(1)}, bf16[32,112]{1,0:T(8,128)(2,1)}, u32[]{:S(2)}) copy-start(bf16[32,112]{1,0:T(8,128)(2,1)} %param.17) | copy-start | bytes 21508
  100.8 9.1 %copy-start.1 = (bf16[1,12288,576]{1,2,0:T(8,128)(2,1)S(1)}, bf16[1,12288,576]{1,2,0:T(8,128)(2,1)}, u32[]{:S(2)}) copy-start(bf16[1,12288,576]{1,2,0:T(8,128)(2,1)} %all-gather.3.cloned.1.call-done) | copy-start | bytes 42467332
  107.2 164.9 %copy-start.2 = (bf16[1,3584,128]{2,1,0:T(8,128)(2,1)S(1)}, bf16[1,3584,128]{2,1,0:T(8,128)(2,1)}, u32[]{:S(2)}) copy-start(bf16[1,3584,128]{2,1,0:T(8,128)(2,1)} %param.19) | copy-start | bytes 2752516
  109.9 189.0 %copy-start.5 = (f32[32,8]{0,1:T(8,128)S(1)}, f32[32,8]{0,1:T(8,128)}, u32[]{:S(2)}) copy-start(f32[32,8]{0,1:T(8,128)} %param.23) | copy-start | bytes 3076
  294.8 13.6 %all-to-all-start.1 = ((f32[32,1,1792]{2,1,0:T(1,128)}), f32[32,1,1792]{2,1,0:T(1,128)S(1)}, u32[]{:S(2)}, u32[]{:S(2)}) async-start(f32[32,1,1792]{2,1,0:T(1,128)} %reshape.195), calls=%async_computation.1 | async-start | bytes 458752 | tf_op jit(solution)/shard_map/all_to_all | solution.py:111
Sparse Core Ops, SparseCore 0:
  9.5 91.2 all-gather.2
where the time goes:
time: 385 us; the launch traced here: 383 us
  blocking collectives  219 us (57%)
  waiting for transfers between devices  98.4 us (26%)
  other arithmetic  21.4 us (6%)
  between operations  14.3 us (4%)
  matrix products  13.3 us (3%)
  local copies, waits for them, and re-layouts  12.6 us (3%)
  starting transfers between devices  4.05 us (1%)
    all_gather x1, waiting for transfers between devices, local(): gathered = lax.all_gather(kv_cache, 'head', axis=1, tiled=True)  90.6 us
    unnamed x1, blocking collectives  61.9 us
    psum x1, blocking collectives, local(): squares = lax.psum(jnp.sum(widened * widened, axis=1), 'expert')  58.4 us
    psum x1, blocking collectives, local(): attn = lax.psum(attn_part, 'head')  52.3 us
    all_gather x1, blocking collectives, local(): lax.all_gather(head_flat, 'expert', axis=0, tiled=True)  34.7 us
    unnamed x1, other arithmetic  17.1 us
    all_to_all x1, blocking collectives, local(): lax.all_to_all(send_rows, 'expert', split_axis=0, concat_axis=2, tiled=True)  12.1 us
    unnamed x19, local copies, waits for them, and re-layouts  11.4 us
  transfers between devices with their start and end apart: 2, of which 2 were waited for; matrix products, arithmetic and copies ran while one was open for 1% of the time, Pallas kernels for 0%

commit v1 on v0

v1 whole, which is shorter than its diff:
```python
import functools

import jax
import jax.numpy as jnp
from jax import lax
from jax.experimental import pallas as pl
from jax.experimental.pallas import tpu as pltpu
from jax.sharding import PartitionSpec as P

LAT = 512
BLK = 64
LANES = 128
NEG = -1e30

score_scale = 192 ** (-0.5)
norm_eps = 1e-06

f32 = jnp.float32
bf16 = jnp.bfloat16


def call(body, out_shape, in_specs, *operands, scratch=()):
    return pl.pallas_call(
        body,
        out_shape=out_shape,
        in_specs=in_specs,
        out_specs=pl.BlockSpec(memory_space=pltpu.VMEM),
        scratch_shapes=scratch,
        compiler_params=pltpu.CompilerParams(vmem_limit_bytes=48 * 1024 * 1024),
    )(*operands)


VM = pl.BlockSpec(memory_space=pltpu.VMEM)
SM = pl.BlockSpec(memory_space=pltpu.SMEM)


def exchange(blocks, axis):
    return lax.all_to_all(blocks, axis, split_axis=0, concat_axis=0, tiled=True)


def attend_body(picks_ref, q_ref, kv_ref, out_ref):
    tokens = kv_ref.shape[0]
    first_block = lax.axis_index("head") * (tokens // BLK)
    block_of = lax.broadcasted_iota(jnp.int32, (8, tokens), 1) // BLK + first_block
    chosen = block_of == picks_ref[0, 0]
    for i in range(1, picks_ref.shape[1]):
        chosen = chosen | (block_of == picks_ref[0, i])
    chosen = chosen[0:1]
    scores = (
        lax.dot_general(q_ref[...], kv_ref[...], (((1,), (1,)), ((), ())), preferred_element_type=f32)
        * score_scale
    )
    scores = jnp.where(chosen, scores, NEG)
    highest = jnp.max(scores, axis=1, keepdims=True)
    top = highest.astype(bf16).astype(f32)
    rest = (highest - top).astype(bf16).astype(f32)
    weights = jnp.where(chosen, jnp.exp(scores - (top + rest)), 0.0)
    total = jnp.sum(weights, axis=1, keepdims=True)
    latent = jnp.dot(weights.astype(bf16), kv_ref[:, :LAT], preferred_element_type=f32)
    total_top = total.astype(bf16).astype(f32)
    total_rest = total - total_top
    lane = lax.broadcasted_iota(jnp.int32, (q_ref.shape[0], LANES), 1)
    stats = jnp.where(
        lane == 0, top, jnp.where(lane == 1, rest, jnp.where(lane == 2, total_top, total_rest))
    )
    out_ref[:, :LAT] = latent.astype(bf16)
    out_ref[:, LAT:] = stats.astype(bf16)


def values_body(parts_ref, uv_ref, gain_ref, out_ref):
    parts = parts_ref[...].astype(f32)
    heads = parts.shape[1]
    stats = parts[:, :, LAT:]
    scale = stats[:, :, 0:1] + stats[:, :, 1:2]
    total = stats[:, :, 2:3] + stats[:, :, 3:4]
    factor = jnp.exp(scale - jnp.max(scale, axis=0, keepdims=True))
    denominator = jnp.sum(factor * total, axis=0)
    attended = jnp.sum(factor * parts[:, :, :LAT], axis=0) / denominator
    row = lax.broadcasted_iota(jnp.int32, attended.shape, 0)
    spread = jnp.concatenate(
        [jnp.where(row == j, attended, 0.0).astype(bf16) for j in range(heads)], axis=1
    )
    head_vals = jnp.dot(spread, uv_ref[...], preferred_element_type=f32)
    gain = gain_ref[...].astype(f32)
    gain = jnp.concatenate([gain, jnp.zeros((1, LANES - gain.shape[1]), f32)], axis=1)
    both = jnp.concatenate([head_vals, jnp.broadcast_to(gain, (8, LANES))], axis=0).astype(bf16)
    out_ref[...] = jnp.broadcast_to(both[None], out_ref.shape)


def project_body(vals_ref, o_ref, out_ref):
    vals = vals_ref[...].astype(f32)
    wide = jnp.concatenate([vals[:, j, :] for j in range(8)], axis=1).astype(bf16)
    part = jnp.dot(wide, o_ref[...], preferred_element_type=f32).astype(bf16)
    part = jnp.concatenate(
        [part, jnp.zeros((part.shape[0], LANES - part.shape[1]), bf16)], axis=1
    )
    out_ref[...] = jnp.broadcast_to(part[None], out_ref.shape)


def mix_body(parts_ref, residual_ref, out_ref):
    attn = jnp.sum(parts_ref[...].astype(f32), axis=0)
    residual = residual_ref[...].astype(f32)
    residual = jnp.concatenate(
        [residual, jnp.zeros((residual.shape[0], LANES - residual.shape[1]), f32)], axis=1
    )
    mixed = (residual + attn).astype(bf16)
    out_ref[...] = jnp.broadcast_to(mixed[None], out_ref.shape)


def expert_body(mixed_ref, vals_ref, gate_ref, up_ref, down_ref, ids_ref, gw_ref, out_ref):
    owners, rows = mixed_ref.shape[:2]
    width = gate_ref.shape[0] // owners
    features = gate_ref.shape[0]
    mixed = mixed_ref[...].astype(f32)
    lane = lax.broadcasted_iota(jnp.int32, (1, 1, LANES), 2)
    mixed = jnp.where(lane < width, mixed, 0.0)
    squares = jnp.sum(jnp.sum(mixed * mixed, axis=0), axis=1, keepdims=True)
    scale = lax.rsqrt(squares / features + norm_eps)
    gain = vals_ref[:, 8:16, :].astype(f32)[:, 0:1, :]
    gain = jnp.where(lane < width, gain, 0.0)
    normed = (mixed * scale[None] * gain).astype(bf16)
    gate_act = jnp.zeros((rows, gate_ref.shape[1]), f32)
    up_act = jnp.zeros((rows, up_ref.shape[1]), f32)
    for i in range(owners):
        mine = normed[i][:, :width]
        gate_act += jnp.dot(mine, gate_ref[i * width : (i + 1) * width, :], preferred_element_type=f32)
        up_act += jnp.dot(mine, up_ref[i * width : (i + 1) * width, :], preferred_element_type=f32)
    hidden = (gate_act / (1.0 + jnp.exp(-gate_act)) * up_act).astype(bf16)
    here = lax.axis_index("expert")
    weight = jnp.sum(jnp.where(ids_ref[...] == here, gw_ref[...], 0.0), axis=1, keepdims=True)
    outcome = jnp.dot(hidden, down_ref[...], preferred_element_type=f32) * weight
    pad = jnp.zeros((rows, LANES - width), f32)
    for i in range(owners):
        out_ref[i] = jnp.concatenate(
            [outcome[:, i * width : (i + 1) * width], pad], axis=1
        ).astype(bf16)


def gather_body(parts_ref, mixed_ref, out_ref):
    share = jnp.sum(parts_ref[...].astype(f32), axis=0)
    first = lax.axis_index("head") == 0
    share = share + jnp.where(first, mixed_ref[0].astype(f32), 0.0)
    groups, rows = out_ref.shape[0], share.shape[0]
    for i in range(groups):
        group = i * rows // groups // 8
        out_ref[i] = share[group * 8 : group * 8 + 8]


def local(
    queries,
    kv_cache,
    block_ids,
    w_uv,
    o_proj,
    residual,
    moe_gain,
    w_gate,
    w_up,
    w_down,
    expert_ids,
    gate_weights,
):
    head_n = lax.axis_size("head")
    expert_n = lax.axis_size("expert")
    heads, width = queries.shape[1:]
    rows = expert_ids.shape[0]
    columns = o_proj.shape[1]
    row_share = rows // head_n

    asked = exchange(jnp.broadcast_to(queries, (head_n, heads, width)), "head")
    shares = call(
        attend_body,
        jax.ShapeDtypeStruct((head_n * heads, LAT + LANES), bf16),
        [SM, VM, VM],
        block_ids,
        asked.reshape(head_n * heads, width),
        kv_cache[0],
    )
    shares = exchange(shares.reshape(head_n, heads, LAT + LANES), "head")
    vals = call(
        values_body,
        jax.ShapeDtypeStruct((expert_n, 16, LANES), bf16),
        [VM, VM, VM],
        shares,
        w_uv.reshape(heads * LAT, -1),
        moe_gain[None, :],
    )
    vals = exchange(vals, "expert")
    attn = call(
        project_body,
        jax.ShapeDtypeStruct((head_n, rows, LANES), bf16),
        [VM, VM],
        vals,
        o_proj,
    )
    attn = exchange(attn, "head")
    mixed = call(
        mix_body,
        jax.ShapeDtypeStruct((expert_n, rows, LANES), bf16),
        [VM, VM],
        attn,
        residual,
    )
    features = exchange(mixed, "expert")
    outcome = call(
        expert_body,
        jax.ShapeDtypeStruct((expert_n, rows, LANES), bf16),
        [VM] * 7,
        features,
        vals,
        w_gate[0],
        w_up[0],
        w_down[0],
        expert_ids,
        gate_weights,
    )
    outcome = exchange(outcome, "expert")
    moe = call(
        gather_body,
        jax.ShapeDtypeStruct((head_n, 8, LANES), f32),
        [VM, VM],
        outcome,
        mixed,
    )
    moe = jnp.sum(exchange(moe, "head"), axis=0)
    first = lax.axis_index("head") * row_share % 8
    return lax.dynamic_slice(moe, (first, 0), (row_share, columns)).astype(bf16)


def solution(mesh):
    in_specs = (
        P("expert", "head", None),
        P("expert", "head", None),
        P("expert", None),
        P("head", None, None),
        P("head", "expert"),
        P(None, "expert"),
        P("expert"),
        P("expert", None, "head"),
        P("expert", None, "head"),
        P("expert", "head", None),
        P(),
        P(),
    )
    out_specs = P("head", "expert")
    return jax.shard_map(local, mesh=mesh, in_specs=in_specs, out_specs=out_specs, check_vma=False)
```

time: 385 us -> 121 us (0.31)
  blocking collectives: 219 us -> 40.5 us
  waiting for transfers between devices: 98.4 us -> 35.9 us
  starting transfers between devices: 4.05 us -> 32.6 us
  other arithmetic: 21.4 us -> 0.02 us
  between operations: 14.3 us -> 0.13 us
  matrix products: 13.3 us -> 0 us
  local copies, waits for them, and re-layouts: 12.6 us -> 5.05 us
  Pallas kernels: 0 us -> 6.27 us
    psum x2 -> x0, blocking collectives: 111 us -> none  [the longest x1 58.4 us: local(): squares = lax.psum(jnp.sum(widened * widened, axis=1), 'expert')]
    all_gather x1 -> x0, waiting for transfers between devices: 90.6 us -> none  [local(): gathered = lax.all_gather(kv_cache, 'head', axis=1, tiled=True)]
    unnamed x1 -> x0, blocking collectives: 61.9 us -> none
    all_gather x1 -> x0, blocking collectives: 34.7 us -> none  [local(): lax.all_gather(head_flat, 'expert', axis=0, tiled=True)]
    all_to_all x1 -> x4, waiting for transfers between devices: 7.08 us -> 35.9 us  [exchange(): return lax.all_to_all(blocks, axis, split_axis=0, concat_axis=0, tiled=True)]
    all_to_all x1 -> x4, starting transfers between devices: 4.05 us -> 32.6 us  [exchange(): return lax.all_to_all(blocks, axis, split_axis=0, concat_axis=0, tiled=True)]
    all_to_all x1 -> x3, blocking collectives: 12.1 us -> 40.5 us  [exchange(): return lax.all_to_all(blocks, axis, split_axis=0, concat_axis=0, tiled=True)]
    unnamed x1 -> x0, other arithmetic: 17.1 us -> none
  transfers between devices with their start and end apart: 2 -> 4, of which waited for: 2 -> 4; matrix products, arithmetic and copies ran while one was open for 1% -> 2% of each run, Pallas kernels for 0% -> 0%
where the time goes in v1:
time: 121 us; the launch traced here: 120 us
  blocking collectives  40.5 us (33%)
  waiting for transfers between devices  35.9 us (30%)
  starting transfers between devices  32.6 us (27%)
  Pallas kernels  6.27 us (5%)
  local copies, waits for them, and re-layouts  5.05 us (4%)
    all_to_all x3, blocking collectives, exchange(): return lax.all_to_all(blocks, axis, split_axis=0, concat_axis=0, tiled=True)  40.5 us
    all_to_all x4, waiting for transfers between devices, exchange(): return lax.all_to_all(blocks, axis, split_axis=0, concat_axis=0, tiled=True)  35.9 us
    all_to_all x4, starting transfers between devices, exchange(): return lax.all_to_all(blocks, axis, split_axis=0, concat_axis=0, tiled=True)  32.6 us
    pallas_call x6, Pallas kernels, call(): pl.pallas_call(body, out_shape=out_shape, in_specs=in_specs, out_specs=pl...  6.27 us
    unnamed x24, local copies, waits for them, and re-layouts  3.16 us
  transfers between devices with their start and end apart: 4, of which 4 were waited for; matrix products, arithmetic and copies ran while one was open for 2% of the time, Pallas kernels for 0%

profile of v1, /device:TPU:1, one launch (start us, length us, event | category | flops | bytes accessed | tf_op | source)
XLA Modules:
  0.0 120.5 jit_solution(10448151278093070566)
XLA Ops:
  0.0 1.4 %broadcast_in_dim.11 = bf16[16,8,576]{2,1,0:T(8,128)(2,1)} broadcast(bf16[8,576]{1,0:T(8,128)(2,1)} %bitcast.17), dimensions={1,2} | broadcast | bytes 156672 | tf_op jit(solution)/shard_map/broadcast_in_dim | solution.py:170
  1.4 10.2 %all-to-all-start = ((bf16[16,8,576]{2,1,0:T(8,128)(2,1)}), bf16[16,8,576]{2,1,0:T(8,128)(2,1)S(1)}, u32[]{:S(2)}, u32[]{:S(2)}) async-start(bf16[16,8,576]{2,1,0:T(8,128)(2,1)} %broadcast_in_dim.11), calls=%async_computation | async-start | bytes 327680 | tf_op jit(solution)/shard_map/all_to_all | solution.py:38
  11.6 0.0 copy-start.6
  11.6 1.5 %copy.13 = bf16[1,768,576]{2,1,0:T(8,128)(2,1)S(1)} copy(bf16[1,768,576]{1,2,0:T(8,128)(2,1)} %param.13) | data formatting | bytes 1769472 | tf_op args[1]
  13.1 0.0 copy-start
  13.1 8.3 %all-to-all-done = bf16[16,8,576]{2,1,0:T(8,128)(2,1)S(1)} async-done(((bf16[16,8,576]{2,1,0:T(8,128)(2,1)}), bf16[16,8,576]{2,1,0:T(8,128)(2,1)S(1)}, u32[]{:S(2)}, u32[]{:S(2)}) %all-to-all-start) | async-done | bytes 147488 | tf_op jit(solution)/shard_map/all_to_all | solution.py:38
  21.5 0.0 copy-done.6
  21.5 1.5 %shard_map.118 = bf16[128,640]{1,0:T(8,128)(2,1)S(1)} custom-call(s32[1,32]{1,0:T(1,128)S(1)} %copy-done.6, bf16[128,576]{1,0:T(8,128)(2,1)S(1)} %bitcast.14, bf16[768,576]{1,0:T(8,128)(2,1)S(1)} %bitcast.9), custom_call_target="tpu_custom_call" | custom-call | tf_op jit(solution)/shard_map/pallas_call | solution.py:23
  22.9 12.1 %all_to_all.35.parts_ref = bf16[16,8,640]{2,1,0:T(8,128)(2,1)S(1)} all-to-all(bf16[16,8,640]{2,1,0:T(8,128)(2,1)S(1)} %bitcast.15), channel_id=1, replica_groups=mesh['expert'=32,'head'=16] {'head'}, dimensions={0} | all-to-all | bytes 327680 | tf_op jit(solution)/shard_map/all_to_all | solution.py:38
  35.0 0.0 copy-start.5
  35.0 0.0 copy-done
  35.0 0.7 copy-done.5
  35.7 0.0 copy-start.3
  35.7 1.1 shard_map.119
  36.8 0.0 copy-start.7
  36.8 11.4 %all-to-all-start.2 = ((bf16[32,16,128]{2,1,0:T(8,128)(2,1)}), bf16[32,16,128]{2,1,0:T(8,128)(2,1)S(1)}, u32[]{:S(2)}, u32[]{:S(2)}) async-start(bf16[32,16,128]{2,1,0:T(8,128)(2,1)} %shard_map.119), calls=%async_computation.2 | async-start | bytes 262144 | tf_op jit(solution)/shard_map/all_to_all | solution.py:38
  48.2 0.0 copy-done.7
  48.2 0.0 copy-start.4
  48.3 0.0 copy-start.2
  48.3 0.2 copy.14.o_ref
  48.4 0.0 copy-start.1
  48.5 9.1 %all-to-all-done.2.vals_ref = bf16[32,16,128]{2,1,0:T(8,128)(2,1)S(1)} async-done(((bf16[32,16,128]{2,1,0:T(8,128)(2,1)}), bf16[32,16,128]{2,1,0:T(8,128)(2,1)S(1)}, u32[]{:S(2)}, u32[]{:S(2)}) %all-to-all-start.2) | async-done | bytes 131104 | tf_op jit(solution)/shard_map/all_to_all | solution.py:38
  57.6 0.2 shard_map.120
  57.8 13.5 %all_to_all.36.parts_ref = bf16[16,32,128]{2,1,0:T(8,128)(2,1)S(1)} all-to-all(bf16[16,32,128]{2,1,0:T(8,128)(2,1)S(1)} %shard_map.120), channel_id=1, replica_groups=mesh['expert'=32,'head'=16] {'head'}, dimensions={0} | all-to-all | bytes 262144 | tf_op jit(solution)/shard_map/all_to_all | solution.py:38
  71.2 0.0 copy-done.4
  71.2 0.7 shard_map.121.mixed_ref
  72.0 0.0 copy-start.8
  72.0 4.0 %all-to-all-start.4 = ((bf16[32,32,128]{2,1,0:T(8,128)(2,1)}), bf16[32,32,128]{2,1,0:T(8,128)(2,1)S(1)}, u32[]{:S(2)}, u32[]{:S(2)}) async-start(bf16[32,32,128]{2,1,0:T(8,128)(2,1)} %shard_map.121.mixed_ref), calls=%async_computation.4 | async-start | bytes 524288 | tf_op jit(solution)/shard_map/all_to_all | solution.py:38
  76.0 0.0 copy-done.8
  76.0 0.0 copy-start.9
  76.0 0.1 copy.15.ids_ref
  76.1 0.6 copy-done.9
  76.7 0.1 copy.16.gw_ref
  76.7 10.7 %all-to-all-done.4.mixed_ref = bf16[32,32,128]{2,1,0:T(8,128)(2,1)S(1)} async-done(((bf16[32,32,128]{2,1,0:T(8,128)(2,1)}), bf16[32,32,128]{2,1,0:T(8,128)(2,1)S(1)}, u32[]{:S(2)}, u32[]{:S(2)}) %all-to-all-start.4) | async-done | bytes 262176 | tf_op jit(solution)/shard_map/all_to_all | solution.py:38
  87.4 0.0 copy-done.3
  87.4 0.0 copy-done.2
  87.4 0.0 copy-done.1
  87.4 1.1 shard_map.122
  88.5 14.9 %all_to_all.37.parts_ref = bf16[32,32,128]{2,1,0:T(8,128)(2,1)S(1)} all-to-all(bf16[32,32,128]{2,1,0:T(8,128)(2,1)S(1)} %shard_map.122), channel_id=1, replica_groups=mesh['expert'=32,'head'=16] {'expert'}, dimensions={0} | all-to-all | bytes 524288 | tf_op jit(solution)/shard_map/all_to_all | solution.py:38
  103.5 1.6 %shard_map.123 = f32[16,8,128]{2,1,0:T(8,128)} custom-call(bf16[32,32,128]{2,1,0:T(8,128)(2,1)S(1)} %all_to_all.37.parts_ref, bf16[32,32,128]{2,1,0:T(8,128)(2,1)} %shard_map.121.mixed_ref), custom_call_target="tpu_custom_call" | custom-call | tf_op jit(solution)/shard_map/pallas_call | solution.py:23
  105.1 7.0 %all-to-all-start.6 = ((f32[16,8,128]{2,1,0:T(8,128)}), f32[16,8,128]{2,1,0:T(8,128)S(1)}, u32[]{:S(2)}, u32[]{:S(2)}) async-start(f32[16,8,128]{2,1,0:T(8,128)} %shard_map.123), calls=%async_computation.6 | async-start | bytes 131072 | tf_op jit(solution)/shard_map/all_to_all | solution.py:38
  112.1 7.8 %all-to-all-done.6 = f32[16,8,128]{2,1,0:T(8,128)S(1)} async-done(((f32[16,8,128]{2,1,0:T(8,128)}), f32[16,8,128]{2,1,0:T(8,128)S(1)}, u32[]{:S(2)}, u32[]{:S(2)}) %all-to-all-start.6) | async-done | bytes 65568 | tf_op jit(solution)/shard_map/all_to_all | solution.py:38
  120.0 0.5 dynamic-slice_convert_fusion
  (1 shorter events, 0.0 us)
Async XLA Ops:
  1.4 20.1 %all-to-all-start = ((bf16[16,8,576]{2,1,0:T(8,128)(2,1)}), bf16[16,8,576]{2,1,0:T(8,128)(2,1)S(1)}, u32[]{:S(2)}, u32[]{:S(2)}) async-start(bf16[16,8,576]{2,1,0:T(8,128)(2,1)} %broadcast_in_dim.11), calls=%async_computation | async-start | bytes 327680 | tf_op jit(solution)/shard_map/all_to_all | solution.py:38
  11.6 9.9 %copy-start.6 = (s32[1,32]{1,0:T(1,128)S(1)}, s32[1,32]{1,0:T(1,128)}, u32[]{:S(2)}) copy-start(s32[1,32]{1,0:T(1,128)} %picks_ref.1) | copy-start | bytes 388
  13.1 21.9 %copy-start = (bf16[8,512,128]{2,1,0:T(8,128)(2,1)S(1)}, bf16[8,512,128]{2,1,0:T(8,128)(2,1)}, u32[]{:S(2)}) copy-start(bf16[8,512,128]{2,1,0:T(8,128)(2,1)} %param.15) | copy-start | bytes 3145732
  35.0 0.7 copy-start.5
  35.7 51.8 %copy-start.3 = (bf16[1,128,3584]{2,1,0:T(8,128)(2,1)S(1)}, bf16[1,128,3584]{2,1,0:T(8,128)(2,1)}, u32[]{:S(2)}) copy-start(bf16[1,128,3584]{2,1,0:T(8,128)(2,1)} %param.21) | copy-start | bytes 2752516
  36.8 11.4 %copy-start.7 = (bf16[1024,112]{0,1:T(8,128)(2,1)S(1)}, bf16[1024,112]{0,1:T(8,128)(2,1)}, u32[]{:S(2)}) copy-start(bf16[1024,112]{0,1:T(8,128)(2,1)} %param.16) | copy-start | bytes 688132
  36.8 20.7 %all-to-all-start.2 = ((bf16[32,16,128]{2,1,0:T(8,128)(2,1)}), bf16[32,16,128]{2,1,0:T(8,128)(2,1)S(1)}, u32[]{:S(2)}, u32[]{:S(2)}) async-start(bf16[32,16,128]{2,1,0:T(8,128)(2,1)} %shard_map.119), calls=%async_computation.2 | async-start | bytes 262144 | tf_op jit(solution)/shard_map/all_to_all | solution.py:38
  48.2 23.0 %copy-start.4 = (bf16[32,112]{1,0:T(8,128)(2,1)S(1)}, bf16[32,112]{1,0:T(8,128)(2,1)}, u32[]{:S(2)}) copy-start(bf16[32,112]{1,0:T(8,128)(2,1)} %residual_ref.1) | copy-start | bytes 21508
  48.3 39.2 %copy-start.2 = (bf16[1,3584,128]{2,1,0:T(8,128)(2,1)S(1)}, bf16[1,3584,128]{2,1,0:T(8,128)(2,1)}, u32[]{:S(2)}) copy-start(bf16[1,3584,128]{2,1,0:T(8,128)(2,1)} %param.20) | copy-start | bytes 2752516
  48.4 39.0 %copy-start.1 = (bf16[1,3584,128]{2,1,0:T(8,128)(2,1)S(1)}, bf16[1,3584,128]{2,1,0:T(8,128)(2,1)}, u32[]{:S(2)}) copy-start(bf16[1,3584,128]{2,1,0:T(8,128)(2,1)} %param.19) | copy-start | bytes 2752516
  72.0 4.0 %copy-start.8 = (s32[32,8]{0,1:T(8,128)S(1)}, s32[32,8]{0,1:T(8,128)}, u32[]{:S(2)}) copy-start(s32[32,8]{0,1:T(8,128)} %param.22) | copy-start | bytes 3076
  72.0 15.5 %all-to-all-start.4 = ((bf16[32,32,128]{2,1,0:T(8,128)(2,1)}), bf16[32,32,128]{2,1,0:T(8,128)(2,1)S(1)}, u32[]{:S(2)}, u32[]{:S(2)}) async-start(bf16[32,32,128]{2,1,0:T(8,128)(2,1)} %shard_map.121.mixed_ref), calls=%async_computation.4 | async-start | bytes 524288 | tf_op jit(solution)/shard_map/all_to_all | solution.py:38
  76.0 0.7 copy-start.9
  105.1 14.8 %all-to-all-start.6 = ((f32[16,8,128]{2,1,0:T(8,128)}), f32[16,8,128]{2,1,0:T(8,128)S(1)}, u32[]{:S(2)}, u32[]{:S(2)}) async-start(f32[16,8,128]{2,1,0:T(8,128)} %shard_map.123), calls=%async_computation.6 | async-start | bytes 131072 | tf_op jit(solution)/shard_map/all_to_all | solution.py:38

commit v2 on v1

v2 whole, which is shorter than its diff:
```python
import functools

import jax
import jax.numpy as jnp
from jax import lax
from jax.experimental import pallas as pl
from jax.experimental.pallas import tpu as pltpu
from jax.sharding import PartitionSpec as P

LAT = 512
BLK = 64
LANES = 128
NEG = -1e30

score_scale = 192 ** (-0.5)
norm_eps = 1e-06

f32 = jnp.float32
bf16 = jnp.bfloat16


VM = pl.BlockSpec(memory_space=pltpu.VMEM)
SM = pl.BlockSpec(memory_space=pltpu.SMEM)
shape = jax.ShapeDtypeStruct


def call(body, out_shape, in_specs, *operands):
    return pl.pallas_call(
        body,
        out_shape=out_shape,
        in_specs=in_specs,
        out_specs=jax.tree.map(lambda _: VM, out_shape),
        compiler_params=pltpu.CompilerParams(vmem_limit_bytes=48 * 1024 * 1024),
    )(*operands)


def exchange(blocks, axis):
    return lax.all_to_all(blocks, axis, split_axis=0, concat_axis=0, tiled=True)


def attend_body(picks_ref, q_ref, kv_ref, out_ref):
    tokens = kv_ref.shape[0]
    first_block = lax.axis_index("head") * (tokens // BLK)
    block_of = lax.broadcasted_iota(jnp.int32, (8, tokens), 1) // BLK + first_block
    chosen = block_of == picks_ref[0, 0]
    for i in range(1, picks_ref.shape[1]):
        chosen = chosen | (block_of == picks_ref[0, i])
    chosen = chosen[0:1]
    scores = (
        lax.dot_general(q_ref[...], kv_ref[...], (((1,), (1,)), ((), ())), preferred_element_type=f32)
        * score_scale
    )
    scores = jnp.where(chosen, scores, NEG)
    highest = jnp.max(scores, axis=1, keepdims=True)
    top = highest.astype(bf16).astype(f32)
    rest = (highest - top).astype(bf16).astype(f32)
    weights = jnp.where(chosen, jnp.exp(scores - (top + rest)), 0.0)
    total = jnp.sum(weights, axis=1, keepdims=True)
    latent = jnp.dot(weights.astype(bf16), kv_ref[:, :LAT], preferred_element_type=f32)
    total_top = total.astype(bf16).astype(f32)
    total_rest = total - total_top
    lane = lax.broadcasted_iota(jnp.int32, (q_ref.shape[0], LANES), 1)
    stats = jnp.where(
        lane == 0, top, jnp.where(lane == 1, rest, jnp.where(lane == 2, total_top, total_rest))
    )
    out_ref[:, :LAT] = latent.astype(bf16)
    out_ref[:, LAT:] = stats.astype(bf16)


def copies_body(one_ref, out_ref):
    out_ref[...] = jnp.broadcast_to(one_ref[...], out_ref.shape)


def tables_body(
    ids_ref, gw_ref, residual_ref, gain_ref, dispatch_ref, combine_ref, weight_ref, residual_out, gain_out
):
    rows, top = ids_ref.shape
    slots = combine_ref.shape[1]
    capacity = weight_ref.shape[0]
    ids = ids_ref[...]
    expert = lax.broadcasted_iota(jnp.int32, (rows, LANES), 1)
    picked = jnp.zeros((rows, LANES), f32)
    for k in range(top):
        picked = picked + (ids[:, k : k + 1] == expert).astype(f32)
    earlier = lax.broadcasted_iota(jnp.int32, (rows, rows), 1) < lax.broadcasted_iota(
        jnp.int32, (rows, rows), 0
    )
    before = jnp.dot(
        earlier.astype(bf16), picked.astype(bf16), preferred_element_type=f32
    )
    held = jnp.where(picked > 0.5, before, -1.0).astype(bf16)
    spread = lax.broadcasted_iota(jnp.int32, (LANES, slots), 0) == (
        lax.broadcasted_iota(jnp.int32, (LANES, slots), 1) // capacity
    )
    along = jnp.dot(held, spread.astype(bf16), preferred_element_type=f32)
    slot = lax.broadcasted_iota(jnp.int32, (rows, slots), 1) % capacity
    combine_ref[...] = (along == slot.astype(f32)).astype(bf16)
    spread = lax.broadcasted_iota(jnp.int32, (slots, LANES), 1) == (
        lax.broadcasted_iota(jnp.int32, (slots, LANES), 0) // capacity
    )
    down = lax.dot_general(
        spread.astype(bf16), held, (((1,), (1,)), ((), ())), preferred_element_type=f32
    )
    slot = lax.broadcasted_iota(jnp.int32, (slots, rows), 0) % capacity
    dispatch_ref[...] = (down == slot.astype(f32)).astype(bf16)
    here = lax.axis_index("expert")
    weight = jnp.sum(jnp.where(ids == here, gw_ref[...], 0.0), axis=1, keepdims=True)
    mine = jnp.sum(
        jnp.where(expert == here, held.astype(f32), 0.0), axis=1, keepdims=True
    )
    by_slot = jnp.sum(jnp.where(mine == expert.astype(f32), weight, 0.0), axis=0, keepdims=True)
    by_slot = jnp.broadcast_to(by_slot, (capacity, LANES))
    diagonal = lax.broadcasted_iota(jnp.int32, (capacity, LANES), 1) == lax.broadcasted_iota(
        jnp.int32, (capacity, LANES), 0
    )
    by_slot = jnp.sum(jnp.where(diagonal, by_slot, 0.0), axis=1, keepdims=True)
    weight_ref[...] = jnp.broadcast_to(by_slot, weight_ref.shape)
    width = residual_ref.shape[1]
    residual_out[...] = jnp.concatenate(
        [residual_ref[...].astype(f32), jnp.zeros((rows, LANES - width), f32)], axis=1
    )
    gain = jnp.concatenate(
        [gain_ref[...].astype(f32), jnp.zeros((1, LANES - width), f32)], axis=1
    )
    gain_out[...] = jnp.broadcast_to(gain, gain_out.shape)


def values_body(parts_ref, uv_ref, out_ref):
    parts = parts_ref[...].astype(f32)
    heads = parts.shape[1]
    stats = parts[:, :, LAT:]
    scale = stats[:, :, 0:1] + stats[:, :, 1:2]
    total = stats[:, :, 2:3] + stats[:, :, 3:4]
    factor = jnp.exp(scale - jnp.max(scale, axis=0, keepdims=True))
    denominator = jnp.sum(factor * total, axis=0)
    attended = jnp.sum(factor * parts[:, :, :LAT], axis=0) / denominator
    row = lax.broadcasted_iota(jnp.int32, attended.shape, 0)
    spread = jnp.concatenate(
        [jnp.where(row == j, attended, 0.0).astype(bf16) for j in range(heads)], axis=1
    )
    head_vals = jnp.dot(spread, uv_ref[...], preferred_element_type=f32).astype(bf16)
    out_ref[...] = jnp.broadcast_to(head_vals[None], out_ref.shape)


def project_body(vals_ref, o_ref, out_ref):
    vals = vals_ref[...].astype(f32)
    wide = jnp.concatenate([vals[:, j, :] for j in range(vals.shape[1])], axis=1).astype(bf16)
    part = jnp.dot(wide, o_ref[...], preferred_element_type=f32).astype(bf16)
    part = jnp.concatenate(
        [part, jnp.zeros((part.shape[0], LANES - part.shape[1]), bf16)], axis=1
    )
    out_ref[...] = jnp.broadcast_to(part[None], out_ref.shape)


def mix_body(width, parts_ref, residual_ref, gain_ref, dispatch_ref, out_ref, mixed_ref):
    attn = jnp.sum(parts_ref[...].astype(f32), axis=0)
    mixed = (residual_ref[...] + attn).astype(bf16).astype(f32)
    mixed_ref[...] = mixed
    squares = jnp.sum(mixed * mixed, axis=1, keepdims=True)
    top = squares.astype(bf16).astype(f32)
    lane = lax.broadcasted_iota(jnp.int32, mixed.shape, 1)
    scaled = jnp.where(
        lane == width, top, jnp.where(lane == width + 1, squares - top, mixed * gain_ref[0:1])
    )
    slots = jnp.dot(dispatch_ref[...], scaled.astype(bf16), preferred_element_type=f32)
    out_ref[...] = slots.astype(bf16).reshape(out_ref.shape)


def expert_body(slots_ref, gate_ref, up_ref, down_ref, weight_ref, out_ref):
    owners, capacity = slots_ref.shape[:2]
    features, units = gate_ref.shape
    width = features // owners
    lane = lax.broadcasted_iota(jnp.int32, (capacity, LANES), 1)
    stats = jnp.sum(slots_ref[...].astype(f32), axis=0)
    stats = jnp.where((lane == width) | (lane == width + 1), stats, 0.0)
    scale = lax.rsqrt(jnp.sum(stats, axis=1, keepdims=True) / features + norm_eps)
    both = jnp.zeros((capacity, 2 * units), f32)
    for i in range(owners):
        part = slice(i * width, (i + 1) * width)
        weights = jnp.concatenate([gate_ref[part, :], up_ref[part, :]], axis=1)
        both += jnp.dot(slots_ref[i][:, :width], weights, preferred_element_type=f32)
    both = both * scale
    gate_act, up_act = both[:, :units], both[:, units:]
    hidden = (gate_act / (1.0 + jnp.exp(-gate_act)) * up_act).astype(bf16)
    outcome = jnp.dot(hidden, down_ref[...], preferred_element_type=f32) * weight_ref[:, 0:1]
    pad = jnp.zeros((capacity, LANES - width), f32)
    for i in range(owners):
        out_ref[i] = jnp.concatenate(
            [outcome[:, i * width : (i + 1) * width], pad], axis=1
        ).astype(bf16)


def gather_body(parts_ref, combine_ref, mixed_ref, out_ref):
    parts = parts_ref[...].reshape(combine_ref.shape[1], LANES)
    share = jnp.dot(combine_ref[...], parts, preferred_element_type=f32)
    share = share + jnp.where(lax.axis_index("head") == 0, mixed_ref[...], 0.0)
    groups, rows = out_ref.shape[0], share.shape[0]
    for i in range(groups):
        group = i * rows // groups // 8
        out_ref[i] = share[group * 8 : group * 8 + 8]


def local(
    queries,
    kv_cache,
    block_ids,
    w_uv,
    o_proj,
    residual,
    moe_gain,
    w_gate,
    w_up,
    w_down,
    expert_ids,
    gate_weights,
):
    head_n = lax.axis_size("head")
    expert_n = lax.axis_size("expert")
    heads, width = queries.shape[1:]
    rows, top = expert_ids.shape
    columns = o_proj.shape[1]
    row_share = rows // head_n
    capacity = min(2 * (rows // expert_n) * top, rows)
    slots = expert_n * capacity

    asked = call(copies_body, shape((head_n, heads, width), bf16), [VM], queries)
    asked = exchange(asked, "head")
    dispatch, combine, weight, residual_wide, gain = call(
        tables_body,
        (
            shape((slots, rows), bf16),
            shape((rows, slots), bf16),
            shape((capacity, LANES), f32),
            shape((rows, LANES), f32),
            shape((8, LANES), f32),
        ),
        [VM] * 4,
        expert_ids,
        gate_weights,
        residual,
        moe_gain[None, :],
    )
    shares = call(
        attend_body,
        shape((head_n * heads, LAT + LANES), bf16),
        [SM, VM, VM],
        block_ids,
        asked.reshape(head_n * heads, width),
        kv_cache[0],
    )
    shares = exchange(shares.reshape(head_n, heads, LAT + LANES), "head")
    vals = call(
        values_body,
        shape((expert_n, heads, w_uv.shape[2]), bf16),
        [VM, VM],
        shares,
        w_uv.reshape(heads * LAT, -1),
    )
    vals = exchange(vals, "expert")
    attn = call(project_body, shape((head_n, rows, LANES), bf16), [VM, VM], vals, o_proj)
    attn = exchange(attn, "head")
    tokens, mixed = call(
        functools.partial(mix_body, columns),
        (shape((expert_n, capacity, LANES), bf16), shape((rows, LANES), f32)),
        [VM] * 4,
        attn,
        residual_wide,
        gain,
        dispatch,
    )
    tokens = exchange(tokens, "expert")
    outcome = call(
        expert_body,
        shape((expert_n, capacity, LANES), bf16),
        [VM] * 5,
        tokens,
        w_gate[0],
        w_up[0],
        w_down[0],
        weight,
    )
    outcome = exchange(outcome, "expert")
    moe = call(gather_body, shape((head_n, 8, LANES), f32), [VM] * 3, outcome, combine, mixed)
    moe = jnp.sum(exchange(moe, "head"), axis=0)
    first = lax.axis_index("head") * row_share % 8
    return lax.dynamic_slice(moe, (first, 0), (row_share, columns)).astype(bf16)


def solution(mesh):
    in_specs = (
        P("expert", "head", None),
        P("expert", "head", None),
        P("expert", None),
        P("head", None, None),
        P("head", "expert"),
        P(None, "expert"),
        P("expert"),
        P("expert", None, "head"),
        P("expert", None, "head"),
        P("expert", "head", None),
        P(),
        P(),
    )
    out_specs = P("head", "expert")
    return jax.shard_map(local, mesh=mesh, in_specs=in_specs, out_specs=out_specs, check_vma=False)
```

time: 121 us -> 114 us (0.942)
  blocking collectives: 40.5 us -> 37.9 us
  waiting for transfers between devices: 35.9 us -> 33.4 us
  local copies, waits for them, and re-layouts: 5.05 us -> 3.13 us
    all_to_all x3, blocking collectives: 40.5 us -> 37.9 us  [exchange(): return lax.all_to_all(blocks, axis, split_axis=0, concat_axis=0, tiled=True)]
    all_to_all x4, waiting for transfers between devices: 35.9 us -> 33.4 us  [exchange(): return lax.all_to_all(blocks, axis, split_axis=0, concat_axis=0, tiled=True)]
    broadcast_in_dim x1 -> x0, local copies, waits for them, and re-layouts: 1.38 us -> none  [local(): asked = exchange(jnp.broadcast_to(queries, (head_n, heads, width)), 'head')]
    unnamed x24 -> x26, local copies, waits for them, and re-layouts: 3.16 us -> 2.61 us
    pallas_call x6 -> x8, Pallas kernels: 6.27 us -> 6.48 us  [call(): pl.pallas_call(body, out_shape=out_shape, in_specs=in_specs, out_specs=ja...]
where the time goes in v2:
time: 114 us; the launch traced here: 113 us
  blocking collectives  37.9 us (33%)
  waiting for transfers between devices  33.4 us (29%)
  starting transfers between devices  31.8 us (28%)
  Pallas kernels  6.48 us (6%)
  local copies, waits for them, and re-layouts  3.13 us (3%)
    all_to_all x3, blocking collectives, exchange(): return lax.all_to_all(blocks, axis, split_axis=0, concat_axis=0, tiled=True)  37.9 us
    all_to_all x4, waiting for transfers between devices, exchange(): return lax.all_to_all(blocks, axis, split_axis=0, concat_axis=0, tiled=True)  33.4 us
    all_to_all x4, starting transfers between devices, exchange(): return lax.all_to_all(blocks, axis, split_axis=0, concat_axis=0, tiled=True)  31.8 us
    pallas_call x8, Pallas kernels, call(): pl.pallas_call(body, out_shape=out_shape, in_specs=in_specs, out_specs=ja...  6.48 us
    unnamed x26, local copies, waits for them, and re-layouts  2.61 us
  transfers between devices with their start and end apart: 4, of which 4 were waited for; matrix products, arithmetic and copies ran while one was open for 2% of the time, Pallas kernels for 0%

profile of v2, /device:TPU:1, one launch (start us, length us, event | category | flops | bytes accessed | tf_op | source)
XLA Modules:
  0.0 112.9 jit_solution(4543350621323228828)
XLA Ops:
  0.0 0.0 copy-start.4
  0.0 0.7 copy-done.4
  0.7 0.7 shard_map.118
  1.4 10.2 %all-to-all-start = ((bf16[16,8,576]{2,1,0:T(8,128)(2,1)}), bf16[16,8,576]{2,1,0:T(8,128)(2,1)S(1)}, u32[]{:S(2)}, u32[]{:S(2)}) async-start(bf16[16,8,576]{2,1,0:T(8,128)(2,1)} %shard_map.118), calls=%async_computation | async-start | bytes 327680 | tf_op jit(solution)/shard_map/all_to_all | solution.py:38
  11.6 0.0 copy-start.6
  11.6 1.5 %copy.13 = bf16[1,768,576]{2,1,0:T(8,128)(2,1)S(1)} copy(bf16[1,768,576]{1,2,0:T(8,128)(2,1)} %param.13) | data formatting | bytes 1769472 | tf_op args[1]
  13.1 0.0 copy-start
  13.1 8.3 %all-to-all-done = bf16[16,8,576]{2,1,0:T(8,128)(2,1)S(1)} async-done(((bf16[16,8,576]{2,1,0:T(8,128)(2,1)}), bf16[16,8,576]{2,1,0:T(8,128)(2,1)S(1)}, u32[]{:S(2)}, u32[]{:S(2)}) %all-to-all-start) | async-done | bytes 147488 | tf_op jit(solution)/shard_map/all_to_all | solution.py:38
  21.5 0.0 copy-done.6
  21.5 1.5 %shard_map.119 = bf16[128,640]{1,0:T(8,128)(2,1)S(1)} custom-call(s32[1,32]{1,0:T(1,128)S(1)} %copy-done.6, bf16[128,576]{1,0:T(8,128)(2,1)S(1)} %bitcast.13, bf16[768,576]{1,0:T(8,128)(2,1)S(1)} %bitcast.8), custom_call_target="tpu_custom_call" | custom-call | tf_op jit(solution)/shard_map/pallas_call | solution.py:28
  22.9 12.1 %all_to_all.35.parts_ref = bf16[16,8,640]{2,1,0:T(8,128)(2,1)S(1)} all-to-all(bf16[16,8,640]{2,1,0:T(8,128)(2,1)S(1)} %bitcast.14), channel_id=1, replica_groups=mesh['expert'=32,'head'=16] {'head'}, dimensions={0} | all-to-all | bytes 327680 | tf_op jit(solution)/shard_map/all_to_all | solution.py:38
  35.0 0.0 copy-done
  35.0 0.0 copy-start.8
  35.0 0.0 copy-start.3
  35.0 1.1 shard_map.120
  36.2 0.0 copy-start.9
  36.2 0.0 copy-start.10
  36.2 0.0 copy-start.5
  36.2 0.0 copy-start.7
  36.2 11.4 %all-to-all-start.2 = ((bf16[32,8,128]{2,1,0:T(8,128)(2,1)}), bf16[32,8,128]{2,1,0:T(8,128)(2,1)S(1)}, u32[]{:S(2)}, u32[]{:S(2)}) async-start(bf16[32,8,128]{2,1,0:T(8,128)(2,1)} %shard_map.120), calls=%async_computation.2 | async-start | bytes 131072 | tf_op jit(solution)/shard_map/all_to_all | solution.py:38
  47.6 0.0 copy-done.8
  47.6 0.0 copy-start.1
  47.6 0.0 copy-start.2
  47.6 0.2 copy.14.o_ref
  47.8 8.7 %all-to-all-done.2.vals_ref = bf16[32,8,128]{2,1,0:T(8,128)(2,1)S(1)} async-done(((bf16[32,8,128]{2,1,0:T(8,128)(2,1)}), bf16[32,8,128]{2,1,0:T(8,128)(2,1)S(1)}, u32[]{:S(2)}, u32[]{:S(2)}) %all-to-all-start.2) | async-done | bytes 65568 | tf_op jit(solution)/shard_map/all_to_all | solution.py:38
  56.5 0.9 shard_map.121
  57.3 4.7 %all-to-all-start.3 = ((bf16[16,32,128]{2,1,0:T(8,128)(2,1)}), bf16[16,32,128]{2,1,0:T(8,128)(2,1)S(1)}, u32[]{:S(2)}, u32[]{:S(2)}) async-start(bf16[16,32,128]{2,1,0:T(8,128)(2,1)} %shard_map.121), calls=%async_computation.3 | async-start | bytes 262144 | tf_op jit(solution)/shard_map/all_to_all | solution.py:38
  62.0 0.0 copy-done.9
  62.0 0.1 copy.15.ids_ref
  62.1 0.0 copy-done.10
  62.1 0.1 copy.16.gw_ref
  62.2 0.0 copy-done.5
  62.2 0.0 copy-done.7
  62.2 0.4 shard_map.122
  62.6 8.6 %all-to-all-done.3.parts_ref = bf16[16,32,128]{2,1,0:T(8,128)(2,1)S(1)} async-done(((bf16[16,32,128]{2,1,0:T(8,128)(2,1)}), bf16[16,32,128]{2,1,0:T(8,128)(2,1)S(1)}, u32[]{:S(2)}, u32[]{:S(2)}) %all-to-all-start.3) | async-done | bytes 131104 | tf_op jit(solution)/shard_map/all_to_all | solution.py:38
  71.3 0.3 shard_map.123
  71.5 12.5 %all_to_all.36.slots_ref = bf16[32,16,128]{2,1,0:T(8,128)(2,1)S(1)} all-to-all(bf16[32,16,128]{2,1,0:T(8,128)(2,1)S(1)} %get-tuple-element.15), channel_id=1, replica_groups=mesh['expert'=32,'head'=16] {'expert'}, dimensions={0} | all-to-all | bytes 262144 | tf_op jit(solution)/shard_map/all_to_all | solution.py:38
  84.0 0.0 copy-done.3
  84.0 0.0 copy-done.1
  84.0 0.0 copy-done.2
  84.0 0.9 shard_map.124
  84.9 13.4 %all_to_all.37.parts_ref = bf16[32,16,128]{2,1,0:T(8,128)(2,1)S(1)} all-to-all(bf16[32,16,128]{2,1,0:T(8,128)(2,1)S(1)} %shard_map.124), channel_id=1, replica_groups=mesh['expert'=32,'head'=16] {'expert'}, dimensions={0} | all-to-all | bytes 262144 | tf_op jit(solution)/shard_map/all_to_all | solution.py:38
  98.3 0.8 shard_map.125
  99.1 5.5 %all-to-all-start.6 = ((f32[16,8,128]{2,1,0:T(8,128)}), f32[16,8,128]{2,1,0:T(8,128)S(1)}, u32[]{:S(2)}, u32[]{:S(2)}) async-start(f32[16,8,128]{2,1,0:T(8,128)} %shard_map.125), calls=%async_computation.6 | async-start | bytes 131072 | tf_op jit(solution)/shard_map/all_to_all | solution.py:38
  104.5 7.8 %all-to-all-done.6 = f32[16,8,128]{2,1,0:T(8,128)S(1)} async-done(((f32[16,8,128]{2,1,0:T(8,128)}), f32[16,8,128]{2,1,0:T(8,128)S(1)}, u32[]{:S(2)}, u32[]{:S(2)}) %all-to-all-start.6) | async-done | bytes 65568 | tf_op jit(solution)/shard_map/all_to_all | solution.py:38
  112.4 0.5 dynamic-slice_convert_fusion
  (1 shorter events, 0.0 us)
Async XLA Ops:
  0.0 0.7 copy-start.4
  1.4 20.1 %all-to-all-start = ((bf16[16,8,576]{2,1,0:T(8,128)(2,1)}), bf16[16,8,576]{2,1,0:T(8,128)(2,1)S(1)}, u32[]{:S(2)}, u32[]{:S(2)}) async-start(bf16[16,8,576]{2,1,0:T(8,128)(2,1)} %shard_map.118), calls=%async_computation | async-start | bytes 327680 | tf_op jit(solution)/shard_map/all_to_all | solution.py:38
  11.6 9.9 %copy-start.6 = (s32[1,32]{1,0:T(1,128)S(1)}, s32[1,32]{1,0:T(1,128)}, u32[]{:S(2)}) copy-start(s32[1,32]{1,0:T(1,128)} %picks_ref.1) | copy-start | bytes 388
  13.1 21.9 %copy-start = (bf16[8,512,128]{2,1,0:T(8,128)(2,1)S(1)}, bf16[8,512,128]{2,1,0:T(8,128)(2,1)}, u32[]{:S(2)}) copy-start(bf16[8,512,128]{2,1,0:T(8,128)(2,1)} %param.15) | copy-start | bytes 3145732
  35.0 12.6 %copy-start.8 = (bf16[1024,112]{0,1:T(8,128)(2,1)S(1)}, bf16[1024,112]{0,1:T(8,128)(2,1)}, u32[]{:S(2)}) copy-start(bf16[1024,112]{0,1:T(8,128)(2,1)} %param.16) | copy-start | bytes 688132
  35.0 49.0 %copy-start.3 = (bf16[1,128,3584]{2,1,0:T(8,128)(2,1)S(1)}, bf16[1,128,3584]{2,1,0:T(8,128)(2,1)}, u32[]{:S(2)}) copy-start(bf16[1,128,3584]{2,1,0:T(8,128)(2,1)} %param.21) | copy-start | bytes 2752516
  36.2 25.9 %copy-start.9 = (s32[32,8]{0,1:T(8,128)S(1)}, s32[32,8]{0,1:T(8,128)}, u32[]{:S(2)}) copy-start(s32[32,8]{0,1:T(8,128)} %param.22) | copy-start | bytes 3076
  36.2 26.0 %copy-start.10 = (f32[32,8]{0,1:T(8,128)S(1)}, f32[32,8]{0,1:T(8,128)}, u32[]{:S(2)}) copy-start(f32[32,8]{0,1:T(8,128)} %param.23) | copy-start | bytes 3076
  36.2 26.0 %copy-start.5 = (bf16[32,112]{1,0:T(8,128)(2,1)S(1)}, bf16[32,112]{1,0:T(8,128)(2,1)}, u32[]{:S(2)}) copy-start(bf16[32,112]{1,0:T(8,128)(2,1)} %residual_ref.1) | copy-start | bytes 21508
  36.2 26.0 %copy-start.7 = (bf16[112]{0:T(256)(128)(2,1)S(1)}, bf16[112]{0:T(256)(128)(2,1)}, u32[]{:S(2)}) copy-start(bf16[112]{0:T(256)(128)(2,1)} %param.18) | copy-start | bytes 676
  36.2 20.3 %all-to-all-start.2 = ((bf16[32,8,128]{2,1,0:T(8,128)(2,1)}), bf16[32,8,128]{2,1,0:T(8,128)(2,1)S(1)}, u32[]{:S(2)}, u32[]{:S(2)}) async-start(bf16[32,8,128]{2,1,0:T(8,128)(2,1)} %shard_map.120), calls=%async_computation.2 | async-start | bytes 131072 | tf_op jit(solution)/shard_map/all_to_all | solution.py:38
  47.6 36.4 %copy-start.1 = (bf16[1,3584,128]{2,1,0:T(8,128)(2,1)S(1)}, bf16[1,3584,128]{2,1,0:T(8,128)(2,1)}, u32[]{:S(2)}) copy-start(bf16[1,3584,128]{2,1,0:T(8,128)(2,1)} %param.19) | copy-start | bytes 2752516
  47.6 36.4 %copy-start.2 = (bf16[1,3584,128]{2,1,0:T(8,128)(2,1)S(1)}, bf16[1,3584,128]{2,1,0:T(8,128)(2,1)}, u32[]{:S(2)}) copy-start(bf16[1,3584,128]{2,1,0:T(8,128)(2,1)} %param.20) | copy-start | bytes 2752516
  57.3 13.9 %all-to-all-start.3 = ((bf16[16,32,128]{2,1,0:T(8,128)(2,1)}), bf16[16,32,128]{2,1,0:T(8,128)(2,1)S(1)}, u32[]{:S(2)}, u32[]{:S(2)}) async-start(bf16[16,32,128]{2,1,0:T(8,128)(2,1)} %shard_map.121), calls=%async_computation.3 | async-start | bytes 262144 | tf_op jit(solution)/shard_map/all_to_all | solution.py:38
  99.1 13.3 %all-to-all-start.6 = ((f32[16,8,128]{2,1,0:T(8,128)}), f32[16,8,128]{2,1,0:T(8,128)S(1)}, u32[]{:S(2)}, u32[]{:S(2)}) async-start(f32[16,8,128]{2,1,0:T(8,128)} %shard_map.125), calls=%async_computation.6 | async-start | bytes 131072 | tf_op jit(solution)/shard_map/all_to_all | solution.py:38

commit v3 on v2

--- a/solution.py
+++ b/solution.py
@@ -38,17 +38,10 @@
     return lax.all_to_all(blocks, axis, split_axis=0, concat_axis=0, tiled=True)
 
 
-def attend_body(picks_ref, q_ref, kv_ref, out_ref):
-    tokens = kv_ref.shape[0]
-    first_block = lax.axis_index("head") * (tokens // BLK)
-    block_of = lax.broadcasted_iota(jnp.int32, (8, tokens), 1) // BLK + first_block
-    chosen = block_of == picks_ref[0, 0]
-    for i in range(1, picks_ref.shape[1]):
-        chosen = chosen | (block_of == picks_ref[0, i])
-    chosen = chosen[0:1]
+def attend_body(chosen_ref, q_ref, kv_ref, out_ref):
+    chosen = chosen_ref[0:1] > 0.5
     scores = (
-        lax.dot_general(q_ref[...], kv_ref[...], (((1,), (1,)), ((), ())), preferred_element_type=f32)
-        * score_scale
+        jnp.dot(q_ref[...], kv_ref[...], preferred_element_type=f32) * score_scale
     )
     scores = jnp.where(chosen, scores, NEG)
     highest = jnp.max(scores, axis=1, keepdims=True)
@@ -56,7 +49,9 @@
     rest = (highest - top).astype(bf16).astype(f32)
     weights = jnp.where(chosen, jnp.exp(scores - (top + rest)), 0.0)
     total = jnp.sum(weights, axis=1, keepdims=True)
-    latent = jnp.dot(weights.astype(bf16), kv_ref[:, :LAT], preferred_element_type=f32)
+    latent = lax.dot_general(
+        weights.astype(bf16), kv_ref[:LAT, :], (((1,), (1,)), ((), ())), preferred_element_type=f32
+    )
     total_top = total.astype(bf16).astype(f32)
     total_rest = total - total_top
     lane = lax.broadcasted_iota(jnp.int32, (q_ref.shape[0], LANES), 1)
@@ -71,13 +66,37 @@
     out_ref[...] = jnp.broadcast_to(one_ref[...], out_ref.shape)
 
 
-def tables_body(
-    ids_ref, gw_ref, residual_ref, gain_ref, dispatch_ref, combine_ref, weight_ref, residual_out, gain_out
+def stage_body(
+    ids_any, gw_any, residual_any, gain_any, picks_any, o_any, cache_any,
+    dispatch_ref, combine_ref, weight_ref, residual_out, gain_out, chosen_ref, o_out, cache_out,
+    ids_ref, gw_ref, residual_ref, gain_ref, picks_ref, o_ref, sems,
 ):
-    rows, top = ids_ref.shape
+    pairs = (
+        (ids_any, ids_ref),
+        (gw_any, gw_ref),
+        (residual_any, residual_ref),
+        (gain_any, gain_ref),
+        (picks_any, picks_ref),
+        (o_any, o_ref),
+        (cache_any, cache_out),
+    )
+    copies = [pltpu.make_async_copy(a, b, sems.at[i]) for i, (a, b) in enumerate(pairs)]
+    for copy in copies:
+        copy.start()
+    for copy in copies:
+        copy.wait()
+    o_out[...] = o_ref[...].T
+    tokens = chosen_ref.shape[1]
+    first_block = lax.axis_index("head") * (tokens // BLK)
+    block_of = lax.broadcasted_iota(jnp.int32, (8, tokens), 1) // BLK + first_block
+    chosen = block_of == picks_ref[0, 0]
+    for i in range(1, picks_ref.shape[1]):
+        chosen = chosen | (block_of == picks_ref[0, i])
+    chosen_ref[...] = chosen.astype(f32)
+    top, rows = ids_ref.shape
     slots = combine_ref.shape[1]
     capacity = weight_ref.shape[0]
-    ids = ids_ref[...]
+    ids = ids_ref[...].T
     expert = lax.broadcasted_iota(jnp.int32, (rows, LANES), 1)
     picked = jnp.zeros((rows, LANES), f32)
     for k in range(top):
@@ -104,7 +123,7 @@
     slot = lax.broadcasted_iota(jnp.int32, (slots, rows), 0) % capacity
     dispatch_ref[...] = (down == slot.astype(f32)).astype(bf16)
     here = lax.axis_index("expert")
-    weight = jnp.sum(jnp.where(ids == here, gw_ref[...], 0.0), axis=1, keepdims=True)
+    weight = jnp.sum(jnp.where(ids == here, gw_ref[...].T, 0.0), axis=1, keepdims=True)
     mine = jnp.sum(
         jnp.where(expert == here, held.astype(f32), 0.0), axis=1, keepdims=True
     )
@@ -200,6 +219,16 @@
         out_ref[i] = share[group * 8 : group * 8 + 8]
 
 
+def finish_body(parts_ref, out_ref):
+    share = jnp.sum(parts_ref[...], axis=0)
+    rows, columns = out_ref.shape
+    place = lax.axis_index("head") % (8 // rows)
+    mine = share[:rows]
+    for i in range(1, 8 // rows):
+        mine = jnp.where(place == i, share[i * rows : (i + 1) * rows], mine)
+    out_ref[...] = mine[:, :columns].astype(bf16)
+
+
 def local(
     queries,
     kv_cache,
@@ -225,28 +254,49 @@
 
     asked = call(copies_body, shape((head_n, heads, width), bf16), [VM], queries)
     asked = exchange(asked, "head")
-    dispatch, combine, weight, residual_wide, gain = call(
-        tables_body,
-        (
+    tokens = kv_cache.shape[1]
+    staged = pl.pallas_call(
+        stage_body,
+        out_shape=(
             shape((slots, rows), bf16),
             shape((rows, slots), bf16),
             shape((capacity, LANES), f32),
             shape((rows, LANES), f32),
             shape((8, LANES), f32),
+            shape((8, tokens), f32),
+            shape(o_proj.shape, bf16),
+            shape((width, tokens), bf16),
         ),
-        [VM] * 4,
-        expert_ids,
-        gate_weights,
+        in_specs=[pl.BlockSpec(memory_space=pl.ANY)] * 7,
+        out_specs=(VM,) * 8,
+        scratch_shapes=[
+            pltpu.VMEM((top, rows), jnp.int32),
+            pltpu.VMEM((top, rows), f32),
+            pltpu.VMEM((rows, columns), bf16),
+            pltpu.VMEM((1, columns), bf16),
+            pltpu.SMEM(block_ids.shape, jnp.int32),
+            pltpu.VMEM((columns, o_proj.shape[0]), bf16),
+            pltpu.SemaphoreType.DMA((7,)),
+        ],
+        compiler_params=pltpu.CompilerParams(vmem_limit_bytes=48 * 1024 * 1024),
+    )(
+        expert_ids.T,
+        gate_weights.T,
         residual,
         moe_gain[None, :],
-    )
+        block_ids,
+        o_proj.T,
+        kv_cache[0].T,
+    )
+    staged, asked = lax.optimization_barrier((staged, asked))
+    dispatch, combine, weight, residual_wide, gain, chosen, o_proj, cache = staged
     shares = call(
         attend_body,
         shape((head_n * heads, LAT + LANES), bf16),
-        [SM, VM, VM],
-        block_ids,
+        [VM] * 3,
+        chosen,
         asked.reshape(head_n * heads, width),
-        kv_cache[0],
+        cache,
     )
     shares = exchange(shares.reshape(head_n, heads, LAT + LANES), "head")
     vals = call(
@@ -281,9 +331,7 @@
     )
     outcome = exchange(outcome, "expert")
     moe = call(gather_body, shape((head_n, 8, LANES), f32), [VM] * 3, outcome, combine, mixed)
-    moe = jnp.sum(exchange(moe, "head"), axis=0)
-    first = lax.axis_index("head") * row_share % 8
-    return lax.dynamic_slice(moe, (first, 0), (row_share, columns)).astype(bf16)
+    return call(finish_body, shape((row_share, columns), bf16), [VM], exchange(moe, "head"))
 
 
 def solution(mesh):

time: 114 us -> 109 us (0.956)
  blocking collectives: 37.9 us -> 83.8 us
  waiting for transfers between devices: 33.4 us -> 6.85 us
  starting transfers between devices: 31.8 us -> 10.3 us
  Pallas kernels: 6.48 us -> 5.05 us
    all_to_all x3 -> x6, blocking collectives: 37.9 us -> 83.8 us  [exchange(): return lax.all_to_all(blocks, axis, split_axis=0, concat_axis=0, tiled=True)]
    all_to_all x4 -> x1, waiting for transfers between devices: 33.4 us -> 6.85 us  [exchange(): return lax.all_to_all(blocks, axis, split_axis=0, concat_axis=0, tiled=True)]
    all_to_all x4 -> x1, starting transfers between devices: 31.8 us -> 10.3 us  [exchange(): return lax.all_to_all(blocks, axis, split_axis=0, concat_axis=0, tiled=True)]
    pallas_call x8, Pallas kernels: 6.48 us -> 3.9 us  [call(): pl.pallas_call(body, out_shape=out_shape, in_specs=in_specs, out_specs=ja...]
    pallas_call x0 -> x1, Pallas kernels: none -> 1.15 us  [local(): pl.pallas_call(stage_body, out_shape=(shape((slots, rows), bf16), shape((...]
    unnamed x26 -> x24, local copies, waits for them, and re-layouts: 2.61 us -> 2.6 us
  transfers between devices with their start and end apart: 4 -> 1, of which waited for: 4 -> 1; matrix products, arithmetic and copies ran while one was open for 2% -> 0% of each run, Pallas kernels for 0% -> 1%
where the time goes in v3:
time: 109 us
  blocking collectives  83.8 us (77%)
  starting transfers between devices  10.3 us (9%)
  waiting for transfers between devices  6.85 us (6%)
  Pallas kernels  5.05 us (5%)
  local copies, waits for them, and re-layouts  2.6 us (2%)
    all_to_all x6, blocking collectives, exchange(): return lax.all_to_all(blocks, axis, split_axis=0, concat_axis=0, tiled=True)  83.8 us
    all_to_all x1, starting transfers between devices, exchange(): return lax.all_to_all(blocks, axis, split_axis=0, concat_axis=0, tiled=True)  10.3 us
    all_to_all x1, waiting for transfers between devices, exchange(): return lax.all_to_all(blocks, axis, split_axis=0, concat_axis=0, tiled=True)  6.85 us
    pallas_call x8, Pallas kernels, call(): pl.pallas_call(body, out_shape=out_shape, in_specs=in_specs, out_specs=ja...  3.9 us
    unnamed x24, local copies, waits for them, and re-layouts  2.6 us
  transfers between devices with their start and end apart: 1, of which 1 were waited for; matrix products, arithmetic and copies ran while one was open for 0% of the time, Pallas kernels for 1%

profile of v3, /device:TPU:1, one launch (start us, length us, event | category | flops | bytes accessed | tf_op | source)
XLA Modules:
  0.0 108.8 jit_solution(14920526086587284822)
XLA Ops:
  0.0 0.0 copy-start.5
  0.0 0.0 copy-start.6
  0.0 0.7 copy-done.6
  0.7 0.7 shard_map.119
  1.4 0.0 copy-start.8
  1.4 0.0 copy-start.9
  1.4 10.3 %all-to-all-start = ((bf16[16,8,576]{2,1,0:T(8,128)(2,1)}), bf16[16,8,576]{2,1,0:T(8,128)(2,1)S(1)}, u32[]{:S(2)}, u32[]{:S(2)}) async-start(bf16[16,8,576]{2,1,0:T(8,128)(2,1)} %shard_map.119), calls=%async_computation | async-start | bytes 327680 | tf_op jit(solution)/shard_map/all_to_all | solution.py:38
  11.7 0.0 copy-start.7
  11.8 0.0 copy-start.10
  11.8 0.0 copy-start.11
  11.8 0.0 copy-done.5
  11.8 0.0 copy-done.8
  11.8 0.0 copy-done.9
  11.8 0.6 copy-done.7
  12.4 0.0 copy-done.10
  12.4 0.0 copy-done.11
  12.4 0.0 copy-start.4
  12.4 1.2 %copy-done.4 = bf16[1,768,576]{1,2,0:T(8,128)(2,1)S(1)} copy-done((bf16[1,768,576]{1,2,0:T(8,128)(2,1)S(1)}, bf16[1,768,576]{1,2,0:T(8,128)(2,1)}, u32[]{:S(2)}) %copy-start.4) | copy-done | bytes 884760
  13.6 1.2 %shard_map.118 = (bf16[512,32]{1,0:T(8,128)(2,1)S(1)}, bf16[32,512]{1,0:T(8,128)(2,1)S(1)}, f32[16,128]{1,0:T(8,128)S(1)}, f32[32,128]{1,0:T(8,128)S(1)}, f32[8,...) custom-call(s32[8,32]{1,0:T(8,128)S(1)} %bitcast.21, ...), custom_call_target="tpu_custom_call" | custom-call | tf_op jit(solution)/shard_map/pallas_call | solution.py:258
  14.8 0.0 copy-start
  14.8 6.8 %all-to-all-done = bf16[16,8,576]{2,1,0:T(8,128)(2,1)S(1)} async-done(((bf16[16,8,576]{2,1,0:T(8,128)(2,1)}), bf16[16,8,576]{2,1,0:T(8,128)(2,1)S(1)}, u32[]{:S(2)}, u32[]{:S(2)}) %all-to-all-start) | async-done | bytes 147488 | tf_op jit(solution)/shard_map/all_to_all | solution.py:38
  21.6 0.7 shard_map.120
  22.4 0.0 copy-start.3
  22.4 12.2 %all_to_all.35.parts_ref = bf16[16,8,640]{2,1,0:T(8,128)(2,1)S(1)} all-to-all(bf16[16,8,640]{2,1,0:T(8,128)(2,1)S(1)} %bitcast.19), channel_id=1, replica_groups=mesh['expert'=32,'head'=16] {'head'}, dimensions={0} | all-to-all | bytes 327680 | tf_op jit(solution)/shard_map/all_to_all | solution.py:38
  34.6 0.0 copy-done
  34.6 0.0 copy-start.2
  34.6 0.5 shard_map.121
  35.1 0.0 copy-start.1
  35.1 20.1 %all_to_all.36.vals_ref = bf16[32,8,128]{2,1,0:T(8,128)(2,1)S(1)} all-to-all(bf16[32,8,128]{2,1,0:T(8,128)(2,1)S(1)} %shard_map.121), channel_id=1, replica_groups=mesh['expert'=32,'head'=16] {'expert'}, dimensions={0} | all-to-all | bytes 131072 | tf_op jit(solution)/shard_map/all_to_all | solution.py:38
  55.2 0.2 shard_map.122
  55.4 13.2 %all_to_all.37.parts_ref = bf16[16,32,128]{2,1,0:T(8,128)(2,1)S(1)} all-to-all(bf16[16,32,128]{2,1,0:T(8,128)(2,1)S(1)} %shard_map.122), channel_id=1, replica_groups=mesh['expert'=32,'head'=16] {'head'}, dimensions={0} | all-to-all | bytes 262144 | tf_op jit(solution)/shard_map/all_to_all | solution.py:38
  68.6 0.3 shard_map.123
  68.9 12.5 %all_to_all.38.slots_ref = bf16[32,16,128]{2,1,0:T(8,128)(2,1)S(1)} all-to-all(bf16[32,16,128]{2,1,0:T(8,128)(2,1)S(1)} %get-tuple-element.39), channel_id=1, replica_groups=mesh['expert'=32,'head'=16] {'expert'}, dimensions={0} | all-to-all | bytes 262144 | tf_op jit(solution)/shard_map/all_to_all | solution.py:38
  81.4 0.0 copy-done.3
  81.4 0.0 copy-done.2
  81.4 0.0 copy-done.1
  81.4 0.9 shard_map.124
  82.3 13.6 %all_to_all.39.parts_ref = bf16[32,16,128]{2,1,0:T(8,128)(2,1)S(1)} all-to-all(bf16[32,16,128]{2,1,0:T(8,128)(2,1)S(1)} %shard_map.124), channel_id=1, replica_groups=mesh['expert'=32,'head'=16] {'expert'}, dimensions={0} | all-to-all | bytes 262144 | tf_op jit(solution)/shard_map/all_to_all | solution.py:38
  95.9 0.1 shard_map.125
  96.0 12.2 %all_to_all.40.parts_ref = f32[16,8,128]{2,1,0:T(8,128)S(1)} all-to-all(f32[16,8,128]{2,1,0:T(8,128)S(1)} %shard_map.125), channel_id=1, replica_groups=mesh['expert'=32,'head'=16] {'head'}, dimensions={0} | all-to-all | bytes 131072 | tf_op jit(solution)/shard_map/all_to_all | solution.py:38
  108.2 0.5 shard_map.126
Async XLA Ops:
  0.0 11.8 %copy-start.5 = (bf16[1024,112]{0,1:T(8,128)(2,1)S(1)}, bf16[1024,112]{0,1:T(8,128)(2,1)}, u32[]{:S(2)}) copy-start(bf16[1024,112]{0,1:T(8,128)(2,1)} %param.16) | copy-start | bytes 688132
  0.0 0.7 copy-start.6
  1.4 10.4 %copy-start.8 = (s32[32,8]{0,1:T(8,128)S(1)}, s32[32,8]{0,1:T(8,128)}, u32[]{:S(2)}) copy-start(s32[32,8]{0,1:T(8,128)} %param.22) | copy-start | bytes 3076
  1.4 10.4 %copy-start.9 = (f32[32,8]{0,1:T(8,128)S(1)}, f32[32,8]{0,1:T(8,128)}, u32[]{:S(2)}) copy-start(f32[32,8]{0,1:T(8,128)} %param.23) | copy-start | bytes 3076
  1.4 20.2 %all-to-all-start = ((bf16[16,8,576]{2,1,0:T(8,128)(2,1)}), bf16[16,8,576]{2,1,0:T(8,128)(2,1)S(1)}, u32[]{:S(2)}, u32[]{:S(2)}) async-start(bf16[16,8,576]{2,1,0:T(8,128)(2,1)} %shard_map.119), calls=%async_computation | async-start | bytes 327680 | tf_op jit(solution)/shard_map/all_to_all | solution.py:38
  11.7 0.7 copy-start.7
  11.8 0.7 copy-start.10
  11.8 0.7 copy-start.11
  12.4 1.2 %copy-start.4 = (bf16[1,768,576]{1,2,0:T(8,128)(2,1)S(1)}, bf16[1,768,576]{1,2,0:T(8,128)(2,1)}, u32[]{:S(2)}) copy-start(bf16[1,768,576]{1,2,0:T(8,128)(2,1)} %param.13) | copy-start | bytes 2654212
  14.8 19.8 %copy-start = (bf16[8,512,128]{2,1,0:T(8,128)(2,1)S(1)}, bf16[8,512,128]{2,1,0:T(8,128)(2,1)}, u32[]{:S(2)}) copy-start(bf16[8,512,128]{2,1,0:T(8,128)(2,1)} %param.15) | copy-start | bytes 3145732
  22.4 59.0 %copy-start.3 = (bf16[1,128,3584]{2,1,0:T(8,128)(2,1)S(1)}, bf16[1,128,3584]{2,1,0:T(8,128)(2,1)}, u32[]{:S(2)}) copy-start(bf16[1,128,3584]{2,1,0:T(8,128)(2,1)} %param.21) | copy-start | bytes 2752516
  34.6 46.8 %copy-start.2 = (bf16[1,3584,128]{2,1,0:T(8,128)(2,1)S(1)}, bf16[1,3584,128]{2,1,0:T(8,128)(2,1)}, u32[]{:S(2)}) copy-start(bf16[1,3584,128]{2,1,0:T(8,128)(2,1)} %param.20) | copy-start | bytes 2752516
  35.1 46.3 %copy-start.1 = (bf16[1,3584,128]{2,1,0:T(8,128)(2,1)S(1)}, bf16[1,3584,128]{2,1,0:T(8,128)(2,1)}, u32[]{:S(2)}) copy-start(bf16[1,3584,128]{2,1,0:T(8,128)(2,1)} %param.19) | copy-start | bytes 2752516

commit v4 on v3

--- a/solution.py
+++ b/solution.py
@@ -34,8 +34,16 @@
     )(*operands)
 
 
+def ring(axis, count):
+    first = count // 2 + 1 if axis == "head" else count * 5 // 8
+    return [(first + i) % count for i in range(count)]
+
+
 def exchange(blocks, axis):
-    return lax.all_to_all(blocks, axis, split_axis=0, concat_axis=0, tiled=True)
+    groups = [ring(axis, blocks.shape[0])]
+    return lax.all_to_all(
+        blocks, axis, split_axis=0, concat_axis=0, tiled=True, axis_index_groups=groups
+    )
 
 
 def attend_body(chosen_ref, q_ref, kv_ref, out_ref):
@@ -62,16 +70,13 @@
     out_ref[:, LAT:] = stats.astype(bf16)
 
 
-def copies_body(one_ref, out_ref):
-    out_ref[...] = jnp.broadcast_to(one_ref[...], out_ref.shape)
-
-
 def stage_body(
-    ids_any, gw_any, residual_any, gain_any, picks_any, o_any, cache_any,
-    dispatch_ref, combine_ref, weight_ref, residual_out, gain_out, chosen_ref, o_out, cache_out,
-    ids_ref, gw_ref, residual_ref, gain_ref, picks_ref, o_ref, sems,
+    queries_any, ids_any, gw_any, residual_any, gain_any, picks_any, o_any, cache_any,
+    copies_out, dispatch_ref, combine_ref, weight_ref, residual_out, gain_out, chosen_ref, o_out, cache_out,
+    query_ref, ids_ref, gw_ref, residual_ref, gain_ref, picks_ref, o_ref, sems,
 ):
     pairs = (
+        (queries_any, query_ref),
         (ids_any, ids_ref),
         (gw_any, gw_ref),
         (residual_any, residual_ref),
@@ -83,9 +88,9 @@
     copies = [pltpu.make_async_copy(a, b, sems.at[i]) for i, (a, b) in enumerate(pairs)]
     for copy in copies:
         copy.start()
-    for copy in copies:
+    for copy in copies[:-2]:
         copy.wait()
-    o_out[...] = o_ref[...].T
+    copies_out[...] = jnp.broadcast_to(query_ref[...], copies_out.shape)
     tokens = chosen_ref.shape[1]
     first_block = lax.axis_index("head") * (tokens // BLK)
     block_of = lax.broadcasted_iota(jnp.int32, (8, tokens), 1) // BLK + first_block
@@ -142,6 +147,9 @@
         [gain_ref[...].astype(f32), jnp.zeros((1, LANES - width), f32)], axis=1
     )
     gain_out[...] = jnp.broadcast_to(gain, gain_out.shape)
+    for copy in copies[-2:]:
+        copy.wait()
+    o_out[...] = o_ref[...].T
 
 
 def values_body(parts_ref, uv_ref, out_ref):
@@ -162,7 +170,8 @@
 
 
 def project_body(vals_ref, o_ref, out_ref):
-    vals = vals_ref[...].astype(f32)
+    order = ring("expert", vals_ref.shape[0])
+    vals = jnp.stack([vals_ref[order.index(i)] for i in range(len(order))]).astype(f32)
     wide = jnp.concatenate([vals[:, j, :] for j in range(vals.shape[1])], axis=1).astype(bf16)
     part = jnp.dot(wide, o_ref[...], preferred_element_type=f32).astype(bf16)
     part = jnp.concatenate(
@@ -182,7 +191,9 @@
         lane == width, top, jnp.where(lane == width + 1, squares - top, mixed * gain_ref[0:1])
     )
     slots = jnp.dot(dispatch_ref[...], scaled.astype(bf16), preferred_element_type=f32)
-    out_ref[...] = slots.astype(bf16).reshape(out_ref.shape)
+    slots = slots.astype(bf16).reshape(out_ref.shape)
+    for i, expert in enumerate(ring("expert", out_ref.shape[0])):
+        out_ref[i] = slots[expert]
 
 
 def expert_body(slots_ref, gate_ref, up_ref, down_ref, weight_ref, out_ref):
@@ -194,8 +205,9 @@
     stats = jnp.where((lane == width) | (lane == width + 1), stats, 0.0)
     scale = lax.rsqrt(jnp.sum(stats, axis=1, keepdims=True) / features + norm_eps)
     both = jnp.zeros((capacity, 2 * units), f32)
-    for i in range(owners):
-        part = slice(i * width, (i + 1) * width)
+    order = ring("expert", owners)
+    for i, owner in enumerate(order):
+        part = slice(owner * width, (owner + 1) * width)
         weights = jnp.concatenate([gate_ref[part, :], up_ref[part, :]], axis=1)
         both += jnp.dot(slots_ref[i][:, :width], weights, preferred_element_type=f32)
     both = both * scale
@@ -203,19 +215,21 @@
     hidden = (gate_act / (1.0 + jnp.exp(-gate_act)) * up_act).astype(bf16)
     outcome = jnp.dot(hidden, down_ref[...], preferred_element_type=f32) * weight_ref[:, 0:1]
     pad = jnp.zeros((capacity, LANES - width), f32)
-    for i in range(owners):
+    for i, owner in enumerate(order):
         out_ref[i] = jnp.concatenate(
-            [outcome[:, i * width : (i + 1) * width], pad], axis=1
+            [outcome[:, owner * width : (owner + 1) * width], pad], axis=1
         ).astype(bf16)
 
 
 def gather_body(parts_ref, combine_ref, mixed_ref, out_ref):
-    parts = parts_ref[...].reshape(combine_ref.shape[1], LANES)
+    order = ring("expert", parts_ref.shape[0])
+    parts = jnp.stack([parts_ref[order.index(i)] for i in range(len(order))])
+    parts = parts.reshape(combine_ref.shape[1], LANES)
     share = jnp.dot(combine_ref[...], parts, preferred_element_type=f32)
     share = share + jnp.where(lax.axis_index("head") == 0, mixed_ref[...], 0.0)
     groups, rows = out_ref.shape[0], share.shape[0]
-    for i in range(groups):
-        group = i * rows // groups // 8
+    for i, owner in enumerate(ring("head", groups)):
+        group = owner * rows // groups // 8
         out_ref[i] = share[group * 8 : group * 8 + 8]
 
 
@@ -252,12 +266,11 @@
     capacity = min(2 * (rows // expert_n) * top, rows)
     slots = expert_n * capacity
 
-    asked = call(copies_body, shape((head_n, heads, width), bf16), [VM], queries)
-    asked = exchange(asked, "head")
     tokens = kv_cache.shape[1]
     staged = pl.pallas_call(
         stage_body,
         out_shape=(
+            shape((head_n, heads, width), bf16),
             shape((slots, rows), bf16),
             shape((rows, slots), bf16),
             shape((capacity, LANES), f32),
@@ -267,29 +280,36 @@
             shape(o_proj.shape, bf16),
             shape((width, tokens), bf16),
         ),
-        in_specs=[pl.BlockSpec(memory_space=pl.ANY)] * 7,
-        out_specs=(VM,) * 8,
+        in_specs=[pl.BlockSpec(memory_space=pltpu.HBM)] * 8,
+        out_specs=(VM,) * 9,
         scratch_shapes=[
+            pltpu.VMEM(queries.shape, bf16),
             pltpu.VMEM((top, rows), jnp.int32),
             pltpu.VMEM((top, rows), f32),
             pltpu.VMEM((rows, columns), bf16),
             pltpu.VMEM((1, columns), bf16),
             pltpu.SMEM(block_ids.shape, jnp.int32),
             pltpu.VMEM((columns, o_proj.shape[0]), bf16),
-            pltpu.SemaphoreType.DMA((7,)),
+            pltpu.SemaphoreType.DMA((8,)),
         ],
         compiler_params=pltpu.CompilerParams(vmem_limit_bytes=48 * 1024 * 1024),
     )(
-        expert_ids.T,
-        gate_weights.T,
-        residual,
-        moe_gain[None, :],
-        block_ids,
-        o_proj.T,
-        kv_cache[0].T,
-    )
-    staged, asked = lax.optimization_barrier((staged, asked))
-    dispatch, combine, weight, residual_wide, gain, chosen, o_proj, cache = staged
+        *(
+            pltpu.with_memory_space_constraint(array, pltpu.HBM)
+            for array in (
+                queries,
+                expert_ids.T,
+                gate_weights.T,
+                residual,
+                moe_gain[None, :],
+                block_ids,
+                o_proj.T,
+                kv_cache[0].T,
+            )
+        )
+    )
+    asked, dispatch, combine, weight, residual_wide, gain, chosen, o_proj, cache = staged
+    asked = exchange(asked, "head")
     shares = call(
         attend_body,
         shape((head_n * heads, LAT + LANES), bf16),

time: 109 us -> 101 us (0.927)
  blocking collectives: 83.8 us -> 95.5 us
  starting transfers between devices: 10.3 us -> 0 us
  waiting for transfers between devices: 6.85 us -> 0 us
  local copies, waits for them, and re-layouts: 2.6 us -> 0.03 us
    all_to_all x6 -> x7, blocking collectives: 83.8 us -> 95.5 us  [exchange(): lax.all_to_all(blocks, axis, split_axis=0, concat_axis=0, tiled=True, axi...]
    all_to_all x1 -> x0, starting transfers between devices: 10.3 us -> none  [exchange(): return lax.all_to_all(blocks, axis, split_axis=0, concat_axis=0, tiled=True)]
    all_to_all x1 -> x0, waiting for transfers between devices: 6.85 us -> none  [exchange(): return lax.all_to_all(blocks, axis, split_axis=0, concat_axis=0, tiled=True)]
    unnamed x24 -> x8, local copies, waits for them, and re-layouts: 2.6 us -> 0.03 us
    pallas_call x8 -> x7, Pallas kernels: 3.9 us -> 3.22 us  [call(): pl.pallas_call(body, out_shape=out_shape, in_specs=in_specs, out_specs=ja...]
  transfers between devices with their start and end apart: 1 -> 0, of which waited for: 1 -> 0; matrix products, arithmetic and copies ran while one was open for 0% -> 0% of each run, Pallas kernels for 1% -> 0%
where the time goes in v4:
time: 101 us; the launch traced here: 100 us
  blocking collectives  95.5 us (95%)
  Pallas kernels  4.78 us (5%)
    all_to_all x7, blocking collectives, exchange(): lax.all_to_all(blocks, axis, split_axis=0, concat_axis=0, tiled=True, axi...  95.5 us
    pallas_call x7, Pallas kernels, call(): pl.pallas_call(body, out_shape=out_shape, in_specs=in_specs, out_specs=ja...  3.22 us

profile of v4, /device:TPU:1, one launch (start us, length us, event | category | flops | bytes accessed | tf_op | source)
XLA Modules:
  0.0 100.3 jit_solution(8511619134855685423)
XLA Ops:
  0.0 1.6 %shard_map.118 = (bf16[16,8,576]{2,1,0:T(8,128)(2,1)S(1)}, bf16[512,32]{1,0:T(8,128)(2,1)S(1)}, bf16[32,512]{1,0:T(8,128)(2,1)S(1)}, f32[16,128]{1,0:T(8,128)S(1...) custom-call(bf16[1,8,576]{2,1,0:T(8,128)(2,1)} %queries_any.1, ...), custom_call_target="tpu_custom_call" | custom-call | tf_op jit(solution)/shard_map/pallas_call | solution.py:270
  1.6 0.0 copy-start
  1.6 18.5 %all_to_all.35 = bf16[16,8,576]{2,1,0:T(8,128)(2,1)S(1)} all-to-all(bf16[16,8,576]{2,1,0:T(8,128)(2,1)S(1)} %get-tuple-element.17), channel_id=1, replica_groups={{9,10,11,12,13,14,15,0,1,2,3,4,5,6,7,8},{25,26,27,28,29,30,31,16,17,18,..., dimensions={0} | all-to-all | bytes 294912 | tf_op jit(solution)/shard_map/all_to_all | solution.py:44
  20.1 0.7 shard_map.119
  20.9 0.0 copy-start.3
  20.9 12.6 %all_to_all.36.parts_ref = bf16[16,8,640]{2,1,0:T(8,128)(2,1)S(1)} all-to-all(bf16[16,8,640]{2,1,0:T(8,128)(2,1)S(1)} %bitcast.18), channel_id=1, replica_groups={{9,10,11,12,13,14,15,0,1,2,3,4,5,6,7,8},{25,26,27,28,29,30,31,16,17,18,..., dimensions={0} | all-to-all | bytes 327680 | tf_op jit(solution)/shard_map/all_to_all | solution.py:44
  33.5 0.0 copy-done
  33.5 0.0 copy-start.2
  33.5 0.5 shard_map.120
  33.9 0.0 copy-start.1
  33.9 14.1 %all_to_all.37.vals_ref = bf16[32,8,128]{2,1,0:T(8,128)(2,1)S(1)} all-to-all(bf16[32,8,128]{2,1,0:T(8,128)(2,1)S(1)} %shard_map.120), channel_id=1, replica_groups={{320,336,352,368,384,400,416,432,448,464,480,496,0,16,32,48,64,80,96,11..., dimensions={0} | all-to-all | bytes 131072 | tf_op jit(solution)/shard_map/all_to_all | solution.py:44
  48.1 0.2 shard_map.121
  48.3 12.4 %all_to_all.38.parts_ref = bf16[16,32,128]{2,1,0:T(8,128)(2,1)S(1)} all-to-all(bf16[16,32,128]{2,1,0:T(8,128)(2,1)S(1)} %shard_map.121), channel_id=1, replica_groups={{9,10,11,12,13,14,15,0,1,2,3,4,5,6,7,8},{25,26,27,28,29,30,31,16,17,18,..., dimensions={0} | all-to-all | bytes 262144 | tf_op jit(solution)/shard_map/all_to_all | solution.py:44
  60.6 0.3 shard_map.122
  60.9 13.9 %all_to_all.39.slots_ref = bf16[32,16,128]{2,1,0:T(8,128)(2,1)S(1)} all-to-all(bf16[32,16,128]{2,1,0:T(8,128)(2,1)S(1)} %get-tuple-element.23), channel_id=1, replica_groups={{320,336,352,368,384,400,416,432,448,464,480,496,0,16,32,48,64,80,96,11..., dimensions={0} | all-to-all | bytes 262144 | tf_op jit(solution)/shard_map/all_to_all | solution.py:44
  74.8 0.0 copy-done.3
  74.8 0.0 copy-done.2
  74.8 0.0 copy-done.1
  74.8 0.9 shard_map.123
  75.7 12.3 %all_to_all.40.parts_ref = bf16[32,16,128]{2,1,0:T(8,128)(2,1)S(1)} all-to-all(bf16[32,16,128]{2,1,0:T(8,128)(2,1)S(1)} %shard_map.123), channel_id=1, replica_groups={{320,336,352,368,384,400,416,432,448,464,480,496,0,16,32,48,64,80,96,11..., dimensions={0} | all-to-all | bytes 262144 | tf_op jit(solution)/shard_map/all_to_all | solution.py:44
  88.1 0.1 shard_map.124
  88.2 11.6 %all_to_all.41.parts_ref = f32[16,8,128]{2,1,0:T(8,128)S(1)} all-to-all(f32[16,8,128]{2,1,0:T(8,128)S(1)} %shard_map.124), channel_id=1, replica_groups={{9,10,11,12,13,14,15,0,1,2,3,4,5,6,7,8},{25,26,27,28,29,30,31,16,17,18,..., dimensions={0} | all-to-all | bytes 131072 | tf_op jit(solution)/shard_map/all_to_all | solution.py:44
  99.8 0.5 shard_map.125
Async XLA Ops:
  1.6 31.9 %copy-start = (bf16[8,512,128]{2,1,0:T(8,128)(2,1)S(1)}, bf16[8,512,128]{2,1,0:T(8,128)(2,1)}, u32[]{:S(2)}) copy-start(bf16[8,512,128]{2,1,0:T(8,128)(2,1)} %param.15) | copy-start | bytes 3145732
  20.9 54.0 %copy-start.3 = (bf16[1,128,3584]{2,1,0:T(8,128)(2,1)S(1)}, bf16[1,128,3584]{2,1,0:T(8,128)(2,1)}, u32[]{:S(2)}) copy-start(bf16[1,128,3584]{2,1,0:T(8,128)(2,1)} %param.21) | copy-start | bytes 2752516
  33.5 41.3 %copy-start.2 = (bf16[1,3584,128]{2,1,0:T(8,128)(2,1)S(1)}, bf16[1,3584,128]{2,1,0:T(8,128)(2,1)}, u32[]{:S(2)}) copy-start(bf16[1,3584,128]{2,1,0:T(8,128)(2,1)} %param.20) | copy-start | bytes 2752516
  33.9 40.9 %copy-start.1 = (bf16[1,3584,128]{2,1,0:T(8,128)(2,1)S(1)}, bf16[1,3584,128]{2,1,0:T(8,128)(2,1)}, u32[]{:S(2)}) copy-start(bf16[1,3584,128]{2,1,0:T(8,128)(2,1)} %param.19) | copy-start | bytes 2752516

commit v5 on v4

--- a/solution.py
+++ b/solution.py
@@ -88,57 +88,44 @@
     copies = [pltpu.make_async_copy(a, b, sems.at[i]) for i, (a, b) in enumerate(pairs)]
     for copy in copies:
         copy.start()
+    top, rows = ids_ref.shape
+    slots = combine_ref.shape[1]
+    capacity = weight_ref.shape[0]
+    experts = slots // capacity
+    expert = lax.broadcasted_iota(jnp.int32, (experts, rows), 0)
+    earlier = lax.broadcasted_iota(jnp.int32, (rows, rows), 0) < lax.broadcasted_iota(
+        jnp.int32, (rows, rows), 1
+    )
+    earlier = earlier.astype(bf16)
     for copy in copies[:-2]:
         copy.wait()
     copies_out[...] = jnp.broadcast_to(query_ref[...], copies_out.shape)
     tokens = chosen_ref.shape[1]
     first_block = lax.axis_index("head") * (tokens // BLK)
-    block_of = lax.broadcasted_iota(jnp.int32, (8, tokens), 1) // BLK + first_block
-    chosen = block_of == picks_ref[0, 0]
-    for i in range(1, picks_ref.shape[1]):
-        chosen = chosen | (block_of == picks_ref[0, i])
-    chosen_ref[...] = chosen.astype(f32)
-    top, rows = ids_ref.shape
-    slots = combine_ref.shape[1]
-    capacity = weight_ref.shape[0]
-    ids = ids_ref[...].T
-    expert = lax.broadcasted_iota(jnp.int32, (rows, LANES), 1)
-    picked = jnp.zeros((rows, LANES), f32)
+    block_of = lax.broadcasted_iota(jnp.int32, (1, tokens), 1) // BLK + first_block
+    count = picks_ref.shape[1]
+    diagonal = lax.broadcasted_iota(jnp.int32, (count, count), 0) == lax.broadcasted_iota(
+        jnp.int32, (count, count), 1
+    )
+    picks = jnp.sum(jnp.where(diagonal, picks_ref[...], 0), axis=1, keepdims=True)
+    chosen = jnp.max((block_of == picks).astype(f32), axis=0, keepdims=True)
+    chosen_ref[...] = jnp.broadcast_to(chosen, chosen_ref.shape)
+    ids = ids_ref[...]
+    picked = jnp.zeros((experts, rows), f32)
     for k in range(top):
-        picked = picked + (ids[:, k : k + 1] == expert).astype(f32)
-    earlier = lax.broadcasted_iota(jnp.int32, (rows, rows), 1) < lax.broadcasted_iota(
-        jnp.int32, (rows, rows), 0
-    )
-    before = jnp.dot(
-        earlier.astype(bf16), picked.astype(bf16), preferred_element_type=f32
-    )
-    held = jnp.where(picked > 0.5, before, -1.0).astype(bf16)
-    spread = lax.broadcasted_iota(jnp.int32, (LANES, slots), 0) == (
-        lax.broadcasted_iota(jnp.int32, (LANES, slots), 1) // capacity
-    )
-    along = jnp.dot(held, spread.astype(bf16), preferred_element_type=f32)
-    slot = lax.broadcasted_iota(jnp.int32, (rows, slots), 1) % capacity
-    combine_ref[...] = (along == slot.astype(f32)).astype(bf16)
-    spread = lax.broadcasted_iota(jnp.int32, (slots, LANES), 1) == (
-        lax.broadcasted_iota(jnp.int32, (slots, LANES), 0) // capacity
-    )
-    down = lax.dot_general(
-        spread.astype(bf16), held, (((1,), (1,)), ((), ())), preferred_element_type=f32
-    )
-    slot = lax.broadcasted_iota(jnp.int32, (slots, rows), 0) % capacity
-    dispatch_ref[...] = (down == slot.astype(f32)).astype(bf16)
+        picked = picked + (ids[k : k + 1, :] == expert).astype(f32)
+    before = jnp.dot(picked.astype(bf16), earlier, preferred_element_type=f32)
+    held = jnp.where(picked > 0.5, before, -1.0)
+    slot = lax.broadcasted_iota(jnp.int32, (experts, capacity, rows), 1).astype(f32)
+    dispatch = (held[:, None, :] == slot).astype(f32).reshape(slots, rows)
+    dispatch_ref[...] = dispatch.astype(bf16)
+    combine_ref[...] = dispatch.T.astype(bf16)
     here = lax.axis_index("expert")
-    weight = jnp.sum(jnp.where(ids == here, gw_ref[...].T, 0.0), axis=1, keepdims=True)
-    mine = jnp.sum(
-        jnp.where(expert == here, held.astype(f32), 0.0), axis=1, keepdims=True
-    )
-    by_slot = jnp.sum(jnp.where(mine == expert.astype(f32), weight, 0.0), axis=0, keepdims=True)
-    by_slot = jnp.broadcast_to(by_slot, (capacity, LANES))
-    diagonal = lax.broadcasted_iota(jnp.int32, (capacity, LANES), 1) == lax.broadcasted_iota(
-        jnp.int32, (capacity, LANES), 0
-    )
-    by_slot = jnp.sum(jnp.where(diagonal, by_slot, 0.0), axis=1, keepdims=True)
-    weight_ref[...] = jnp.broadcast_to(by_slot, weight_ref.shape)
+    weight = jnp.sum(jnp.where(ids == here, gw_ref[...], 0.0), axis=0, keepdims=True)
+    mine = jnp.sum(jnp.where(expert == here, held, 0.0), axis=0, keepdims=True)
+    slot = lax.broadcasted_iota(jnp.int32, (capacity, rows), 0).astype(f32)
+    weight = jnp.sum(jnp.where(mine == slot, weight, 0.0), axis=1, keepdims=True)
+    weight_ref[...] = jnp.broadcast_to(weight, weight_ref.shape)
     width = residual_ref.shape[1]
     residual_out[...] = jnp.concatenate(
         [residual_ref[...].astype(f32), jnp.zeros((rows, LANES - width), f32)], axis=1
@@ -149,7 +136,7 @@
     gain_out[...] = jnp.broadcast_to(gain, gain_out.shape)
     for copy in copies[-2:]:
         copy.wait()
-    o_out[...] = o_ref[...].T
+    o_out[...] = o_ref[...]
 
 
 def values_body(parts_ref, uv_ref, out_ref):
@@ -173,7 +160,9 @@
     order = ring("expert", vals_ref.shape[0])
     vals = jnp.stack([vals_ref[order.index(i)] for i in range(len(order))]).astype(f32)
     wide = jnp.concatenate([vals[:, j, :] for j in range(vals.shape[1])], axis=1).astype(bf16)
-    part = jnp.dot(wide, o_ref[...], preferred_element_type=f32).astype(bf16)
+    part = lax.dot_general(
+        wide, o_ref[...], (((1,), (1,)), ((), ())), preferred_element_type=f32
+    ).astype(bf16)
     part = jnp.concatenate(
         [part, jnp.zeros((part.shape[0], LANES - part.shape[1]), bf16)], axis=1
     )
@@ -204,14 +193,12 @@
     stats = jnp.sum(slots_ref[...].astype(f32), axis=0)
     stats = jnp.where((lane == width) | (lane == width + 1), stats, 0.0)
     scale = lax.rsqrt(jnp.sum(stats, axis=1, keepdims=True) / features + norm_eps)
-    both = jnp.zeros((capacity, 2 * units), f32)
     order = ring("expert", owners)
-    for i, owner in enumerate(order):
-        part = slice(owner * width, (owner + 1) * width)
-        weights = jnp.concatenate([gate_ref[part, :], up_ref[part, :]], axis=1)
-        both += jnp.dot(slots_ref[i][:, :width], weights, preferred_element_type=f32)
-    both = both * scale
-    gate_act, up_act = both[:, :units], both[:, units:]
+    wide = jnp.concatenate(
+        [slots_ref[order.index(i)][:, :width] for i in range(owners)], axis=1
+    )
+    gate_act = jnp.dot(wide, gate_ref[...], preferred_element_type=f32) * scale
+    up_act = jnp.dot(wide, up_ref[...], preferred_element_type=f32) * scale
     hidden = (gate_act / (1.0 + jnp.exp(-gate_act)) * up_act).astype(bf16)
     outcome = jnp.dot(hidden, down_ref[...], preferred_element_type=f32) * weight_ref[:, 0:1]
     pad = jnp.zeros((capacity, LANES - width), f32)
@@ -277,7 +264,7 @@
             shape((rows, LANES), f32),
             shape((8, LANES), f32),
             shape((8, tokens), f32),
-            shape(o_proj.shape, bf16),
+            shape(o_proj.shape[::-1], bf16),
             shape((width, tokens), bf16),
         ),
         in_specs=[pl.BlockSpec(memory_space=pltpu.HBM)] * 8,
@@ -288,7 +275,7 @@
             pltpu.VMEM((top, rows), f32),
             pltpu.VMEM((rows, columns), bf16),
             pltpu.VMEM((1, columns), bf16),
-            pltpu.SMEM(block_ids.shape, jnp.int32),
+            pltpu.VMEM(block_ids.shape, jnp.int32),
             pltpu.VMEM((columns, o_proj.shape[0]), bf16),
             pltpu.SemaphoreType.DMA((8,)),
         ],

time: 101 us -> 100 us (0.990)
  no operation moved by 1% of the time
where the time goes in v5:
time: 100 us
  blocking collectives  95.4 us (95%)
  Pallas kernels  4.5 us (4%)
    all_to_all x7, blocking collectives, exchange(): lax.all_to_all(blocks, axis, split_axis=0, concat_axis=0, tiled=True, axi...  95.4 us
    pallas_call x7, Pallas kernels, call(): pl.pallas_call(body, out_shape=out_shape, in_specs=in_specs, out_specs=ja...  3.04 us

profile of v5, /device:TPU:1, one launch (start us, length us, event | category | flops | bytes accessed | tf_op | source)
XLA Modules:
  0.0 100.0 jit_solution(413065887833819098)
XLA Ops:
  0.0 1.5 %shard_map.118 = (bf16[16,8,576]{2,1,0:T(8,128)(2,1)S(1)}, bf16[512,32]{1,0:T(8,128)(2,1)S(1)}, bf16[32,512]{1,0:T(8,128)(2,1)S(1)}, f32[16,128]{1,0:T(8,128)S(1...) custom-call(bf16[1,8,576]{2,1,0:T(8,128)(2,1)} %queries_any.1, ...), custom_call_target="tpu_custom_call" | custom-call | tf_op jit(solution)/shard_map/pallas_call | solution.py:257
  1.5 0.0 copy-start
  1.5 18.5 %all_to_all.35 = bf16[16,8,576]{2,1,0:T(8,128)(2,1)S(1)} all-to-all(bf16[16,8,576]{2,1,0:T(8,128)(2,1)S(1)} %get-tuple-element.17), channel_id=1, replica_groups={{9,10,11,12,13,14,15,0,1,2,3,4,5,6,7,8},{25,26,27,28,29,30,31,16,17,18,..., dimensions={0} | all-to-all | bytes 294912 | tf_op jit(solution)/shard_map/all_to_all | solution.py:44
  20.0 0.7 shard_map.119
  20.8 0.0 copy-start.3
  20.8 12.6 %all_to_all.36.parts_ref = bf16[16,8,640]{2,1,0:T(8,128)(2,1)S(1)} all-to-all(bf16[16,8,640]{2,1,0:T(8,128)(2,1)S(1)} %bitcast.18), channel_id=1, replica_groups={{9,10,11,12,13,14,15,0,1,2,3,4,5,6,7,8},{25,26,27,28,29,30,31,16,17,18,..., dimensions={0} | all-to-all | bytes 327680 | tf_op jit(solution)/shard_map/all_to_all | solution.py:44
  33.4 0.0 copy-done
  33.4 0.0 copy-start.2
  33.4 0.5 shard_map.120
  33.8 0.0 copy-start.1
  33.9 14.1 %all_to_all.37.vals_ref = bf16[32,8,128]{2,1,0:T(8,128)(2,1)S(1)} all-to-all(bf16[32,8,128]{2,1,0:T(8,128)(2,1)S(1)} %shard_map.120), channel_id=1, replica_groups={{320,336,352,368,384,400,416,432,448,464,480,496,0,16,32,48,64,80,96,11..., dimensions={0} | all-to-all | bytes 131072 | tf_op jit(solution)/shard_map/all_to_all | solution.py:44
  48.0 0.2 shard_map.121
  48.2 12.4 %all_to_all.38.parts_ref = bf16[16,32,128]{2,1,0:T(8,128)(2,1)S(1)} all-to-all(bf16[16,32,128]{2,1,0:T(8,128)(2,1)S(1)} %shard_map.121), channel_id=1, replica_groups={{9,10,11,12,13,14,15,0,1,2,3,4,5,6,7,8},{25,26,27,28,29,30,31,16,17,18,..., dimensions={0} | all-to-all | bytes 262144 | tf_op jit(solution)/shard_map/all_to_all | solution.py:44
  60.6 0.3 shard_map.122
  60.8 13.9 %all_to_all.39.slots_ref = bf16[32,16,128]{2,1,0:T(8,128)(2,1)S(1)} all-to-all(bf16[32,16,128]{2,1,0:T(8,128)(2,1)S(1)} %get-tuple-element.23), channel_id=1, replica_groups={{320,336,352,368,384,400,416,432,448,464,480,496,0,16,32,48,64,80,96,11..., dimensions={0} | all-to-all | bytes 262144 | tf_op jit(solution)/shard_map/all_to_all | solution.py:44
  74.7 0.0 copy-done.3
  74.7 0.0 copy-done.2
  74.7 0.0 copy-done.1
  74.7 0.7 shard_map.123
  75.4 12.3 %all_to_all.40.parts_ref = bf16[32,16,128]{2,1,0:T(8,128)(2,1)S(1)} all-to-all(bf16[32,16,128]{2,1,0:T(8,128)(2,1)S(1)} %shard_map.123), channel_id=1, replica_groups={{320,336,352,368,384,400,416,432,448,464,480,496,0,16,32,48,64,80,96,11..., dimensions={0} | all-to-all | bytes 262144 | tf_op jit(solution)/shard_map/all_to_all | solution.py:44
  87.8 0.1 shard_map.124
  87.9 11.6 %all_to_all.41.parts_ref = f32[16,8,128]{2,1,0:T(8,128)S(1)} all-to-all(f32[16,8,128]{2,1,0:T(8,128)S(1)} %shard_map.124), channel_id=1, replica_groups={{9,10,11,12,13,14,15,0,1,2,3,4,5,6,7,8},{25,26,27,28,29,30,31,16,17,18,..., dimensions={0} | all-to-all | bytes 131072 | tf_op jit(solution)/shard_map/all_to_all | solution.py:44
  99.5 0.5 shard_map.125
Async XLA Ops:
  1.5 31.9 %copy-start = (bf16[8,512,128]{2,1,0:T(8,128)(2,1)S(1)}, bf16[8,512,128]{2,1,0:T(8,128)(2,1)}, u32[]{:S(2)}) copy-start(bf16[8,512,128]{2,1,0:T(8,128)(2,1)} %param.15) | copy-start | bytes 3145732
  20.8 54.0 %copy-start.3 = (bf16[1,128,3584]{2,1,0:T(8,128)(2,1)S(1)}, bf16[1,128,3584]{2,1,0:T(8,128)(2,1)}, u32[]{:S(2)}) copy-start(bf16[1,128,3584]{2,1,0:T(8,128)(2,1)} %param.21) | copy-start | bytes 2752516
  33.4 41.3 %copy-start.2 = (bf16[1,3584,128]{2,1,0:T(8,128)(2,1)S(1)}, bf16[1,3584,128]{2,1,0:T(8,128)(2,1)}, u32[]{:S(2)}) copy-start(bf16[1,3584,128]{2,1,0:T(8,128)(2,1)} %param.20) | copy-start | bytes 2752516
  33.8 40.9 %copy-start.1 = (bf16[1,3584,128]{2,1,0:T(8,128)(2,1)S(1)}, bf16[1,3584,128]{2,1,0:T(8,128)(2,1)}, u32[]{:S(2)}) copy-start(bf16[1,3584,128]{2,1,0:T(8,128)(2,1)} %param.19) | copy-start | bytes 2752516

commit v6 on v5

--- a/solution.py
+++ b/solution.py
@@ -39,26 +39,35 @@
     return [(first + i) % count for i in range(count)]
 
 
-def exchange(blocks, axis):
-    groups = [ring(axis, blocks.shape[0])]
+def exchange(blocks, axis, groups=None):
+    groups = groups or [ring(axis, blocks.shape[0])]
     return lax.all_to_all(
         blocks, axis, split_axis=0, concat_axis=0, tiled=True, axis_index_groups=groups
     )
 
 
-def attend_body(chosen_ref, q_ref, kv_ref, out_ref):
+def attend_body(chosen_ref, q_ref, mine_ref, other_ref, out_ref):
+    caches = (mine_ref, other_ref)
     chosen = chosen_ref[0:1] > 0.5
-    scores = (
-        jnp.dot(q_ref[...], kv_ref[...], preferred_element_type=f32) * score_scale
-    )
-    scores = jnp.where(chosen, scores, NEG)
+    scores = jnp.concatenate(
+        [jnp.dot(q_ref[...], ref[...], preferred_element_type=f32) for ref in caches], axis=1
+    )
+    scores = jnp.where(chosen, scores * score_scale, NEG)
     highest = jnp.max(scores, axis=1, keepdims=True)
     top = highest.astype(bf16).astype(f32)
     rest = (highest - top).astype(bf16).astype(f32)
     weights = jnp.where(chosen, jnp.exp(scores - (top + rest)), 0.0)
     total = jnp.sum(weights, axis=1, keepdims=True)
-    latent = lax.dot_general(
-        weights.astype(bf16), kv_ref[:LAT, :], (((1,), (1,)), ((), ())), preferred_element_type=f32
+    weights = weights.astype(bf16)
+    tokens = mine_ref.shape[1]
+    latent = sum(
+        lax.dot_general(
+            weights[:, i * tokens : (i + 1) * tokens],
+            ref[:LAT, :],
+            (((1,), (1,)), ((), ())),
+            preferred_element_type=f32,
+        )
+        for i, ref in enumerate(caches)
     )
     total_top = total.astype(bf16).astype(f32)
     total_rest = total - total_top
@@ -100,9 +109,12 @@
     for copy in copies[:-2]:
         copy.wait()
     copies_out[...] = jnp.broadcast_to(query_ref[...], copies_out.shape)
-    tokens = chosen_ref.shape[1]
-    first_block = lax.axis_index("head") * (tokens // BLK)
-    block_of = lax.broadcasted_iota(jnp.int32, (1, tokens), 1) // BLK + first_block
+    tokens = chosen_ref.shape[1] // 2
+    here = lax.axis_index("head")
+    there = here + 1 - 2 * (here % 2)
+    place = lax.broadcasted_iota(jnp.int32, (1, 2 * tokens), 1) // BLK
+    blocks = tokens // BLK
+    block_of = place + jnp.where(place < blocks, here * blocks, (there - 1) * blocks)
     count = picks_ref.shape[1]
     diagonal = lax.broadcasted_iota(jnp.int32, (count, count), 0) == lax.broadcasted_iota(
         jnp.int32, (count, count), 1
@@ -254,16 +266,19 @@
     slots = expert_n * capacity
 
     tokens = kv_cache.shape[1]
+    chips = head_n // 2
+    alike = [[(head_n // 2 + 2 * i + core) % head_n for i in range(chips)] for core in (0, 1)]
+    other = lax.ppermute(kv_cache[0].T, "head", [(i, i ^ 1) for i in range(head_n)])
     staged = pl.pallas_call(
         stage_body,
         out_shape=(
-            shape((head_n, heads, width), bf16),
+            shape((chips, heads, width), bf16),
             shape((slots, rows), bf16),
             shape((rows, slots), bf16),
             shape((capacity, LANES), f32),
             shape((rows, LANES), f32),
             shape((8, LANES), f32),
-            shape((8, tokens), f32),
+            shape((8, 2 * tokens), f32),
             shape(o_proj.shape[::-1], bf16),
             shape((width, tokens), bf16),
         ),
@@ -296,16 +311,17 @@
         )
     )
     asked, dispatch, combine, weight, residual_wide, gain, chosen, o_proj, cache = staged
-    asked = exchange(asked, "head")
+    asked = exchange(asked, "head", alike)
     shares = call(
         attend_body,
-        shape((head_n * heads, LAT + LANES), bf16),
-        [VM] * 3,
+        shape((chips * heads, LAT + LANES), bf16),
+        [VM] * 4,
         chosen,
-        asked.reshape(head_n * heads, width),
+        asked.reshape(chips * heads, width),
         cache,
-    )
-    shares = exchange(shares.reshape(head_n, heads, LAT + LANES), "head")
+        other,
+    )
+    shares = exchange(shares.reshape(chips, heads, LAT + LANES), "head", alike)
     vals = call(
         values_body,
         shape((expert_n, heads, w_uv.shape[2]), bf16),

time: 100 us -> 99.8 us (level)
  blocking collectives: 95.4 us -> 85.7 us
  starting transfers between devices: 0 us -> 8.77 us
    all_to_all x7, blocking collectives: 95.4 us -> 85.7 us  [exchange(): lax.all_to_all(blocks, axis, split_axis=0, concat_axis=0, tiled=True, axi...]
    ppermute x0 -> x1, starting transfers between devices: none -> 8.77 us  [local(): lax.ppermute(kv_cache[0].T, 'head', [(i, i ^ 1) for i in range(head_n)])]
  transfers between devices with their start and end apart: 0 -> 1, of which waited for: 0 -> 0; matrix products, arithmetic and copies ran while one was open for 0% -> 0% of each run, Pallas kernels for 0% -> 1%
where the time goes in v6:
time: 99.8 us; the launch traced here: 99.4 us
  blocking collectives  85.7 us (86%)
  starting transfers between devices  8.77 us (9%)
  Pallas kernels  4.84 us (5%)
    all_to_all x7, blocking collectives, exchange(): lax.all_to_all(blocks, axis, split_axis=0, concat_axis=0, tiled=True, axi...  85.7 us
    ppermute x1, starting transfers between devices, local(): lax.ppermute(kv_cache[0].T, 'head', [(i, i ^ 1) for i in range(head_n)])  8.77 us
    pallas_call x7, Pallas kernels, call(): pl.pallas_call(body, out_shape=out_shape, in_specs=in_specs, out_specs=ja...  3.37 us
  transfers between devices with their start and end apart: 1, of which 0 were waited for; matrix products, arithmetic and copies ran while one was open for 0% of the time, Pallas kernels for 1%

profile of v6, /device:TPU:1, one launch (start us, length us, event | category | flops | bytes accessed | tf_op | source)
XLA Modules:
  0.0 99.4 jit_solution(2506158706936563418)
XLA Ops:
  0.0 8.8 %collective-permute-start = (bf16[576,768]{1,0:T(8,128)(2,1)}, bf16[576,768]{1,0:T(8,128)(2,1)S(1)}, u32[]{:S(2)}, u32[]{:S(2)}) collective-permute-start(bf16[576,768]{1,0:T(8,128)(2,1)} %bitcast.19), channel_id=1, source_target_pairs={{0,1},{1,0},{2,3},{3,2},{4,5},{5,4},{6,7},{7,6},{8,9},{9,8},{10,11... | collective-permute-start | bytes 2654216 | tf_op jit(solution)/shard_map/ppermute | solution.py:271
  8.8 1.5 %shard_map.118 = (bf16[8,8,576]{2,1,0:T(8,128)(2,1)S(1)}, bf16[512,32]{1,0:T(8,128)(2,1)S(1)}, bf16[32,512]{1,0:T(8,128)(2,1)S(1)}, f32[16,128]{1,0:T(8,128)S(1)...) custom-call(bf16[1,8,576]{2,1,0:T(8,128)(2,1)} %queries_any.1, ...), custom_call_target="tpu_custom_call" | custom-call | tf_op jit(solution)/shard_map/pallas_call | solution.py:272
  10.3 9.4 %all_to_all.35 = bf16[8,8,576]{2,1,0:T(8,128)(2,1)S(1)} all-to-all(bf16[8,8,576]{2,1,0:T(8,128)(2,1)S(1)} %get-tuple-element.17), channel_id=1, replica_groups={{8,10,12,14,0,2,4,6},{9,11,13,15,1,3,5,7},{24,26,28,30,16,18,20,22},{25..., dimensions={0} | all-to-all | bytes 147456 | tf_op jit(solution)/shard_map/all_to_all | solution.py:44
  19.6 0.0 collective-permute-done.other_ref
  19.6 0.0 copy-start
  19.6 0.0 copy-start.3
  19.6 1.1 %shard_map.119 = bf16[64,640]{1,0:T(8,128)(2,1)S(1)} custom-call(f32[8,1536]{1,0:T(8,128)S(1)} %get-tuple-element.16.chosen_ref, bf16[64,576]{1,0:T(8,128)(2,1)S(1)} %bitcast.17, bf16[576,768]{1,0:T(8,128)(2,1)S(1)} %get-tuple-element.18.mine_ref, bf16[576,768]{1,0:T(8,128)(2,1)S(1)} %collective-permute-done.other_ref), custom_call_target="tpu_custom_call" | custom-call | tf_op jit(solution)/shard_map/pallas_call | solution.py:28
  20.7 9.4 %all_to_all.36.parts_ref = bf16[8,8,640]{2,1,0:T(8,128)(2,1)S(1)} all-to-all(bf16[8,8,640]{2,1,0:T(8,128)(2,1)S(1)} %bitcast.18), channel_id=1, replica_groups={{8,10,12,14,0,2,4,6},{9,11,13,15,1,3,5,7},{24,26,28,30,16,18,20,22},{25..., dimensions={0} | all-to-all | bytes 163840 | tf_op jit(solution)/shard_map/all_to_all | solution.py:44
  30.1 0.0 copy-done
  30.1 0.0 copy-start.2
  30.1 0.4 shard_map.120
  30.6 0.0 copy-start.1
  30.6 15.0 %all_to_all.37.vals_ref = bf16[32,8,128]{2,1,0:T(8,128)(2,1)S(1)} all-to-all(bf16[32,8,128]{2,1,0:T(8,128)(2,1)S(1)} %shard_map.120), channel_id=1, replica_groups={{320,336,352,368,384,400,416,432,448,464,480,496,0,16,32,48,64,80,96,11..., dimensions={0} | all-to-all | bytes 131072 | tf_op jit(solution)/shard_map/all_to_all | solution.py:44
  45.6 0.2 shard_map.121
  45.8 14.0 %all_to_all.38.parts_ref = bf16[16,32,128]{2,1,0:T(8,128)(2,1)S(1)} all-to-all(bf16[16,32,128]{2,1,0:T(8,128)(2,1)S(1)} %shard_map.121), channel_id=1, replica_groups={{9,10,11,12,13,14,15,0,1,2,3,4,5,6,7,8},{25,26,27,28,29,30,31,16,17,18,..., dimensions={0} | all-to-all | bytes 262144 | tf_op jit(solution)/shard_map/all_to_all | solution.py:44
  59.8 0.3 shard_map.122
  60.1 13.9 %all_to_all.39.slots_ref = bf16[32,16,128]{2,1,0:T(8,128)(2,1)S(1)} all-to-all(bf16[32,16,128]{2,1,0:T(8,128)(2,1)S(1)} %get-tuple-element.23), channel_id=1, replica_groups={{320,336,352,368,384,400,416,432,448,464,480,496,0,16,32,48,64,80,96,11..., dimensions={0} | all-to-all | bytes 262144 | tf_op jit(solution)/shard_map/all_to_all | solution.py:44
  74.0 0.0 copy-done.3
  74.0 0.0 copy-done.2
  74.0 0.0 copy-done.1
  74.1 0.7 shard_map.123
  74.8 12.3 %all_to_all.40.parts_ref = bf16[32,16,128]{2,1,0:T(8,128)(2,1)S(1)} all-to-all(bf16[32,16,128]{2,1,0:T(8,128)(2,1)S(1)} %shard_map.123), channel_id=1, replica_groups={{320,336,352,368,384,400,416,432,448,464,480,496,0,16,32,48,64,80,96,11..., dimensions={0} | all-to-all | bytes 262144 | tf_op jit(solution)/shard_map/all_to_all | solution.py:44
  87.1 0.1 shard_map.124
  87.2 11.6 %all_to_all.41.parts_ref = f32[16,8,128]{2,1,0:T(8,128)S(1)} all-to-all(f32[16,8,128]{2,1,0:T(8,128)S(1)} %shard_map.124), channel_id=1, replica_groups={{9,10,11,12,13,14,15,0,1,2,3,4,5,6,7,8},{25,26,27,28,29,30,31,16,17,18,..., dimensions={0} | all-to-all | bytes 131072 | tf_op jit(solution)/shard_map/all_to_all | solution.py:44
  98.8 0.5 shard_map.125
Async XLA Ops:
  0.0 19.6 %collective-permute-start = (bf16[576,768]{1,0:T(8,128)(2,1)}, bf16[576,768]{1,0:T(8,128)(2,1)S(1)}, u32[]{:S(2)}, u32[]{:S(2)}) collective-permute-start(bf16[576,768]{1,0:T(8,128)(2,1)} %bitcast.19), channel_id=1, source_target_pairs={{0,1},{1,0},{2,3},{3,2},{4,5},{5,4},{6,7},{7,6},{8,9},{9,8},{10,11... | collective-permute-start | bytes 2654216 | tf_op jit(solution)/shard_map/ppermute | solution.py:271
  19.6 10.5 %copy-start = (bf16[8,512,128]{2,1,0:T(8,128)(2,1)S(1)}, bf16[8,512,128]{2,1,0:T(8,128)(2,1)}, u32[]{:S(2)}) copy-start(bf16[8,512,128]{2,1,0:T(8,128)(2,1)} %param.15) | copy-start | bytes 3145732
  19.6 54.4 %copy-start.3 = (bf16[1,128,3584]{2,1,0:T(8,128)(2,1)S(1)}, bf16[1,128,3584]{2,1,0:T(8,128)(2,1)}, u32[]{:S(2)}) copy-start(bf16[1,128,3584]{2,1,0:T(8,128)(2,1)} %param.21) | copy-start | bytes 2752516
  30.1 43.9 %copy-start.2 = (bf16[1,3584,128]{2,1,0:T(8,128)(2,1)S(1)}, bf16[1,3584,128]{2,1,0:T(8,128)(2,1)}, u32[]{:S(2)}) copy-start(bf16[1,3584,128]{2,1,0:T(8,128)(2,1)} %param.20) | copy-start | bytes 2752516
  30.6 43.5 %copy-start.1 = (bf16[1,3584,128]{2,1,0:T(8,128)(2,1)S(1)}, bf16[1,3584,128]{2,1,0:T(8,128)(2,1)}, u32[]{:S(2)}) copy-start(bf16[1,3584,128]{2,1,0:T(8,128)(2,1)} %param.19) | copy-start | bytes 2752516

commit v7 on v6

--- a/solution.py
+++ b/solution.py
@@ -35,7 +35,7 @@
 
 
 def ring(axis, count):
-    first = count // 2 + 1 if axis == "head" else count * 5 // 8
+    first = count // 2 + 3 if axis == "head" else count * 11 // 16
     return [(first + i) % count for i in range(count)]
 
 
@@ -267,7 +267,7 @@
 
     tokens = kv_cache.shape[1]
     chips = head_n // 2
-    alike = [[(head_n // 2 + 2 * i + core) % head_n for i in range(chips)] for core in (0, 1)]
+    alike = [[(head_n // 2 + 2 + 2 * i + core) % head_n for i in range(chips)] for core in (0, 1)]
     other = lax.ppermute(kv_cache[0].T, "head", [(i, i ^ 1) for i in range(head_n)])
     staged = pl.pallas_call(
         stage_body,

time: 99.8 us -> 99.6 us (level)
  no operation moved by 1% of the time
where the time goes in v7:
time: 99.6 us; the launch traced here: 99.1 us
  blocking collectives  85.5 us (86%)
  starting transfers between devices  8.77 us (9%)
  Pallas kernels  4.83 us (5%)
    all_to_all x7, blocking collectives, exchange(): lax.all_to_all(blocks, axis, split_axis=0, concat_axis=0, tiled=True, axi...  85.5 us
    ppermute x1, starting transfers between devices, local(): lax.ppermute(kv_cache[0].T, 'head', [(i, i ^ 1) for i in range(head_n)])  8.77 us
    pallas_call x7, Pallas kernels, call(): pl.pallas_call(body, out_shape=out_shape, in_specs=in_specs, out_specs=ja...  3.37 us
  transfers between devices with their start and end apart: 1, of which 0 were waited for; matrix products, arithmetic and copies ran while one was open for 0% of the time, Pallas kernels for 1%

profile of v7, /device:TPU:1, one launch (start us, length us, event | category | flops | bytes accessed | tf_op | source)
XLA Modules:
  0.0 99.1 jit_solution(660989793420451035)
XLA Ops:
  0.0 8.8 %collective-permute-start = (bf16[576,768]{1,0:T(8,128)(2,1)}, bf16[576,768]{1,0:T(8,128)(2,1)S(1)}, u32[]{:S(2)}, u32[]{:S(2)}) collective-permute-start(bf16[576,768]{1,0:T(8,128)(2,1)} %bitcast.19), channel_id=1, source_target_pairs={{0,1},{1,0},{2,3},{3,2},{4,5},{5,4},{6,7},{7,6},{8,9},{9,8},{10,11... | collective-permute-start | bytes 2654216 | tf_op jit(solution)/shard_map/ppermute | solution.py:271
  8.8 1.5 %shard_map.118 = (bf16[8,8,576]{2,1,0:T(8,128)(2,1)S(1)}, bf16[512,32]{1,0:T(8,128)(2,1)S(1)}, bf16[32,512]{1,0:T(8,128)(2,1)S(1)}, f32[16,128]{1,0:T(8,128)S(1)...) custom-call(bf16[1,8,576]{2,1,0:T(8,128)(2,1)} %queries_any.1, ...), custom_call_target="tpu_custom_call" | custom-call | tf_op jit(solution)/shard_map/pallas_call | solution.py:272
  10.3 9.4 %all_to_all.35 = bf16[8,8,576]{2,1,0:T(8,128)(2,1)S(1)} all-to-all(bf16[8,8,576]{2,1,0:T(8,128)(2,1)S(1)} %get-tuple-element.17), channel_id=1, replica_groups={{10,12,14,0,2,4,6,8},{11,13,15,1,3,5,7,9},{26,28,30,16,18,20,22,24},{27..., dimensions={0} | all-to-all | bytes 147456 | tf_op jit(solution)/shard_map/all_to_all | solution.py:44
  19.6 0.0 collective-permute-done.other_ref
  19.6 0.0 copy-start
  19.6 0.0 copy-start.3
  19.6 1.1 %shard_map.119 = bf16[64,640]{1,0:T(8,128)(2,1)S(1)} custom-call(f32[8,1536]{1,0:T(8,128)S(1)} %get-tuple-element.16.chosen_ref, bf16[64,576]{1,0:T(8,128)(2,1)S(1)} %bitcast.17, bf16[576,768]{1,0:T(8,128)(2,1)S(1)} %get-tuple-element.18.mine_ref, bf16[576,768]{1,0:T(8,128)(2,1)S(1)} %collective-permute-done.other_ref), custom_call_target="tpu_custom_call" | custom-call | tf_op jit(solution)/shard_map/pallas_call | solution.py:28
  20.7 9.1 %all_to_all.36.parts_ref = bf16[8,8,640]{2,1,0:T(8,128)(2,1)S(1)} all-to-all(bf16[8,8,640]{2,1,0:T(8,128)(2,1)S(1)} %bitcast.18), channel_id=1, replica_groups={{10,12,14,0,2,4,6,8},{11,13,15,1,3,5,7,9},{26,28,30,16,18,20,22,24},{27..., dimensions={0} | all-to-all | bytes 163840 | tf_op jit(solution)/shard_map/all_to_all | solution.py:44
  29.8 0.0 copy-done
  29.8 0.0 copy-start.2
  29.8 0.4 shard_map.120
  30.2 0.0 copy-start.1
  30.3 14.7 %all_to_all.37.vals_ref = bf16[32,8,128]{2,1,0:T(8,128)(2,1)S(1)} all-to-all(bf16[32,8,128]{2,1,0:T(8,128)(2,1)S(1)} %shard_map.120), channel_id=1, replica_groups={{352,368,384,400,416,432,448,464,480,496,0,16,32,48,64,80,96,112,128,14..., dimensions={0} | all-to-all | bytes 131072 | tf_op jit(solution)/shard_map/all_to_all | solution.py:44
  44.9 0.2 shard_map.121
  45.1 14.5 %all_to_all.38.parts_ref = bf16[16,32,128]{2,1,0:T(8,128)(2,1)S(1)} all-to-all(bf16[16,32,128]{2,1,0:T(8,128)(2,1)S(1)} %shard_map.121), channel_id=1, replica_groups={{11,12,13,14,15,0,1,2,3,4,5,6,7,8,9,10},{27,28,29,30,31,16,17,18,19,20,..., dimensions={0} | all-to-all | bytes 262144 | tf_op jit(solution)/shard_map/all_to_all | solution.py:44
  59.6 0.3 shard_map.122
  59.9 12.9 %all_to_all.39.slots_ref = bf16[32,16,128]{2,1,0:T(8,128)(2,1)S(1)} all-to-all(bf16[32,16,128]{2,1,0:T(8,128)(2,1)S(1)} %get-tuple-element.23), channel_id=1, replica_groups={{352,368,384,400,416,432,448,464,480,496,0,16,32,48,64,80,96,112,128,14..., dimensions={0} | all-to-all | bytes 262144 | tf_op jit(solution)/shard_map/all_to_all | solution.py:44
  72.8 0.0 copy-done.3
  72.8 0.0 copy-done.2
  72.8 0.0 copy-done.1
  72.8 0.7 shard_map.123
  73.5 13.2 %all_to_all.40.parts_ref = bf16[32,16,128]{2,1,0:T(8,128)(2,1)S(1)} all-to-all(bf16[32,16,128]{2,1,0:T(8,128)(2,1)S(1)} %shard_map.123), channel_id=1, replica_groups={{352,368,384,400,416,432,448,464,480,496,0,16,32,48,64,80,96,112,128,14..., dimensions={0} | all-to-all | bytes 262144 | tf_op jit(solution)/shard_map/all_to_all | solution.py:44
  86.7 0.1 shard_map.124
  86.8 11.8 %all_to_all.41.parts_ref = f32[16,8,128]{2,1,0:T(8,128)S(1)} all-to-all(f32[16,8,128]{2,1,0:T(8,128)S(1)} %shard_map.124), channel_id=1, replica_groups={{11,12,13,14,15,0,1,2,3,4,5,6,7,8,9,10},{27,28,29,30,31,16,17,18,19,20,..., dimensions={0} | all-to-all | bytes 131072 | tf_op jit(solution)/shard_map/all_to_all | solution.py:44
  98.6 0.5 shard_map.125
Async XLA Ops:
  0.0 19.6 %collective-permute-start = (bf16[576,768]{1,0:T(8,128)(2,1)}, bf16[576,768]{1,0:T(8,128)(2,1)S(1)}, u32[]{:S(2)}, u32[]{:S(2)}) collective-permute-start(bf16[576,768]{1,0:T(8,128)(2,1)} %bitcast.19), channel_id=1, source_target_pairs={{0,1},{1,0},{2,3},{3,2},{4,5},{5,4},{6,7},{7,6},{8,9},{9,8},{10,11... | collective-permute-start | bytes 2654216 | tf_op jit(solution)/shard_map/ppermute | solution.py:271
  19.6 10.1 %copy-start = (bf16[8,512,128]{2,1,0:T(8,128)(2,1)S(1)}, bf16[8,512,128]{2,1,0:T(8,128)(2,1)}, u32[]{:S(2)}) copy-start(bf16[8,512,128]{2,1,0:T(8,128)(2,1)} %param.15) | copy-start | bytes 3145732
  19.6 53.1 %copy-start.3 = (bf16[1,128,3584]{2,1,0:T(8,128)(2,1)S(1)}, bf16[1,128,3584]{2,1,0:T(8,128)(2,1)}, u32[]{:S(2)}) copy-start(bf16[1,128,3584]{2,1,0:T(8,128)(2,1)} %param.21) | copy-start | bytes 2752516
  29.8 43.0 %copy-start.2 = (bf16[1,3584,128]{2,1,0:T(8,128)(2,1)S(1)}, bf16[1,3584,128]{2,1,0:T(8,128)(2,1)}, u32[]{:S(2)}) copy-start(bf16[1,3584,128]{2,1,0:T(8,128)(2,1)} %param.20) | copy-start | bytes 2752516
  30.2 42.5 %copy-start.1 = (bf16[1,3584,128]{2,1,0:T(8,128)(2,1)S(1)}, bf16[1,3584,128]{2,1,0:T(8,128)(2,1)}, u32[]{:S(2)}) copy-start(bf16[1,3584,128]{2,1,0:T(8,128)(2,1)} %param.19) | copy-start | bytes 2752516

commit v8 on v7

--- a/solution.py
+++ b/solution.py
@@ -82,16 +82,16 @@
 def stage_body(
     queries_any, ids_any, gw_any, residual_any, gain_any, picks_any, o_any, cache_any,
     copies_out, dispatch_ref, combine_ref, weight_ref, residual_out, gain_out, chosen_ref, o_out, cache_out,
-    query_ref, ids_ref, gw_ref, residual_ref, gain_ref, picks_ref, o_ref, sems,
+    ids_ref, gw_ref, residual_ref, gain_ref, picks_ref, sems,
 ):
     pairs = (
-        (queries_any, query_ref),
+        (queries_any, copies_out.at[pl.ds(0, 1)]),
         (ids_any, ids_ref),
         (gw_any, gw_ref),
         (residual_any, residual_ref),
         (gain_any, gain_ref),
         (picks_any, picks_ref),
-        (o_any, o_ref),
+        (o_any, o_out),
         (cache_any, cache_out),
     )
     copies = [pltpu.make_async_copy(a, b, sems.at[i]) for i, (a, b) in enumerate(pairs)]
@@ -108,7 +108,8 @@
     earlier = earlier.astype(bf16)
     for copy in copies[:-2]:
         copy.wait()
-    copies_out[...] = jnp.broadcast_to(query_ref[...], copies_out.shape)
+    others = copies_out.shape[0] - 1
+    copies_out[1:] = jnp.broadcast_to(copies_out[0:1], (others,) + copies_out.shape[1:])
     tokens = chosen_ref.shape[1] // 2
     here = lax.axis_index("head")
     there = here + 1 - 2 * (here % 2)
@@ -148,7 +149,6 @@
     gain_out[...] = jnp.broadcast_to(gain, gain_out.shape)
     for copy in copies[-2:]:
         copy.wait()
-    o_out[...] = o_ref[...]
 
 
 def values_body(parts_ref, uv_ref, out_ref):
@@ -285,13 +285,11 @@
         in_specs=[pl.BlockSpec(memory_space=pltpu.HBM)] * 8,
         out_specs=(VM,) * 9,
         scratch_shapes=[
-            pltpu.VMEM(queries.shape, bf16),
             pltpu.VMEM((top, rows), jnp.int32),
             pltpu.VMEM((top, rows), f32),
             pltpu.VMEM((rows, columns), bf16),
             pltpu.VMEM((1, columns), bf16),
             pltpu.VMEM(block_ids.shape, jnp.int32),
-            pltpu.VMEM((columns, o_proj.shape[0]), bf16),
             pltpu.SemaphoreType.DMA((8,)),
         ],
         compiler_params=pltpu.CompilerParams(vmem_limit_bytes=48 * 1024 * 1024),

time: 99.6 us -> 99.6 us (level)
  no operation moved by 1% of the time
where the time goes in v8:
time: 99.6 us; the launch traced here: 99.1 us
  blocking collectives  85.4 us (86%)
  starting transfers between devices  8.77 us (9%)
  Pallas kernels  4.83 us (5%)
    all_to_all x7, blocking collectives, exchange(): lax.all_to_all(blocks, axis, split_axis=0, concat_axis=0, tiled=True, axi...  85.4 us
    ppermute x1, starting transfers between devices, local(): lax.ppermute(kv_cache[0].T, 'head', [(i, i ^ 1) for i in range(head_n)])  8.77 us
    pallas_call x7, Pallas kernels, call(): pl.pallas_call(body, out_shape=out_shape, in_specs=in_specs, out_specs=ja...  3.37 us
  transfers between devices with their start and end apart: 1, of which 0 were waited for; matrix products, arithmetic and copies ran while one was open for 0% of the time, Pallas kernels for 1%

profile of v8, /device:TPU:1, one launch (start us, length us, event | category | flops | bytes accessed | tf_op | source)
XLA Modules:
  0.0 99.1 jit_solution(5408893630510501337)
XLA Ops:
  0.0 8.8 %collective-permute-start = (bf16[576,768]{1,0:T(8,128)(2,1)}, bf16[576,768]{1,0:T(8,128)(2,1)S(1)}, u32[]{:S(2)}, u32[]{:S(2)}) collective-permute-start(bf16[576,768]{1,0:T(8,128)(2,1)} %bitcast.19), channel_id=1, source_target_pairs={{0,1},{1,0},{2,3},{3,2},{4,5},{5,4},{6,7},{7,6},{8,9},{9,8},{10,11... | collective-permute-start | bytes 2654216 | tf_op jit(solution)/shard_map/ppermute | solution.py:271
  8.8 1.5 %shard_map.118 = (bf16[8,8,576]{2,1,0:T(8,128)(2,1)S(1)}, bf16[512,32]{1,0:T(8,128)(2,1)S(1)}, bf16[32,512]{1,0:T(8,128)(2,1)S(1)}, f32[16,128]{1,0:T(8,128)S(1)...) custom-call(bf16[1,8,576]{2,1,0:T(8,128)(2,1)} %queries_any.1, ...), custom_call_target="tpu_custom_call" | custom-call | tf_op jit(solution)/shard_map/pallas_call | solution.py:272
  10.2 9.4 %all_to_all.35 = bf16[8,8,576]{2,1,0:T(8,128)(2,1)S(1)} all-to-all(bf16[8,8,576]{2,1,0:T(8,128)(2,1)S(1)} %get-tuple-element.17), channel_id=1, replica_groups={{10,12,14,0,2,4,6,8},{11,13,15,1,3,5,7,9},{26,28,30,16,18,20,22,24},{27..., dimensions={0} | all-to-all | bytes 147456 | tf_op jit(solution)/shard_map/all_to_all | solution.py:44
  19.6 0.0 collective-permute-done.other_ref
  19.6 0.0 copy-start
  19.6 0.0 copy-start.3
  19.6 1.1 %shard_map.119 = bf16[64,640]{1,0:T(8,128)(2,1)S(1)} custom-call(f32[8,1536]{1,0:T(8,128)S(1)} %get-tuple-element.16.chosen_ref, bf16[64,576]{1,0:T(8,128)(2,1)S(1)} %bitcast.17, bf16[576,768]{1,0:T(8,128)(2,1)S(1)} %get-tuple-element.18.mine_ref, bf16[576,768]{1,0:T(8,128)(2,1)S(1)} %collective-permute-done.other_ref), custom_call_target="tpu_custom_call" | custom-call | tf_op jit(solution)/shard_map/pallas_call | solution.py:28
  20.7 9.1 %all_to_all.36.parts_ref = bf16[8,8,640]{2,1,0:T(8,128)(2,1)S(1)} all-to-all(bf16[8,8,640]{2,1,0:T(8,128)(2,1)S(1)} %bitcast.18), channel_id=1, replica_groups={{10,12,14,0,2,4,6,8},{11,13,15,1,3,5,7,9},{26,28,30,16,18,20,22,24},{27..., dimensions={0} | all-to-all | bytes 163840 | tf_op jit(solution)/shard_map/all_to_all | solution.py:44
  29.8 0.0 copy-done
  29.8 0.0 copy-start.2
  29.8 0.4 shard_map.120
  30.2 0.0 copy-start.1
  30.2 14.6 %all_to_all.37.vals_ref = bf16[32,8,128]{2,1,0:T(8,128)(2,1)S(1)} all-to-all(bf16[32,8,128]{2,1,0:T(8,128)(2,1)S(1)} %shard_map.120), channel_id=1, replica_groups={{352,368,384,400,416,432,448,464,480,496,0,16,32,48,64,80,96,112,128,14..., dimensions={0} | all-to-all | bytes 131072 | tf_op jit(solution)/shard_map/all_to_all | solution.py:44
  44.9 0.2 shard_map.121
  45.1 14.5 %all_to_all.38.parts_ref = bf16[16,32,128]{2,1,0:T(8,128)(2,1)S(1)} all-to-all(bf16[16,32,128]{2,1,0:T(8,128)(2,1)S(1)} %shard_map.121), channel_id=1, replica_groups={{11,12,13,14,15,0,1,2,3,4,5,6,7,8,9,10},{27,28,29,30,31,16,17,18,19,20,..., dimensions={0} | all-to-all | bytes 262144 | tf_op jit(solution)/shard_map/all_to_all | solution.py:44
  59.6 0.3 shard_map.122
  59.8 12.9 %all_to_all.39.slots_ref = bf16[32,16,128]{2,1,0:T(8,128)(2,1)S(1)} all-to-all(bf16[32,16,128]{2,1,0:T(8,128)(2,1)S(1)} %get-tuple-element.23), channel_id=1, replica_groups={{352,368,384,400,416,432,448,464,480,496,0,16,32,48,64,80,96,112,128,14..., dimensions={0} | all-to-all | bytes 262144 | tf_op jit(solution)/shard_map/all_to_all | solution.py:44
  72.7 0.0 copy-done.3
  72.7 0.0 copy-done.2
  72.7 0.0 copy-done.1
  72.8 0.7 shard_map.123
  73.5 13.2 %all_to_all.40.parts_ref = bf16[32,16,128]{2,1,0:T(8,128)(2,1)S(1)} all-to-all(bf16[32,16,128]{2,1,0:T(8,128)(2,1)S(1)} %shard_map.123), channel_id=1, replica_groups={{352,368,384,400,416,432,448,464,480,496,0,16,32,48,64,80,96,112,128,14..., dimensions={0} | all-to-all | bytes 262144 | tf_op jit(solution)/shard_map/all_to_all | solution.py:44
  86.7 0.1 shard_map.124
  86.8 11.8 %all_to_all.41.parts_ref = f32[16,8,128]{2,1,0:T(8,128)S(1)} all-to-all(f32[16,8,128]{2,1,0:T(8,128)S(1)} %shard_map.124), channel_id=1, replica_groups={{11,12,13,14,15,0,1,2,3,4,5,6,7,8,9,10},{27,28,29,30,31,16,17,18,19,20,..., dimensions={0} | all-to-all | bytes 131072 | tf_op jit(solution)/shard_map/all_to_all | solution.py:44
  98.6 0.5 shard_map.125
Async XLA Ops:
  0.0 19.6 %collective-permute-start = (bf16[576,768]{1,0:T(8,128)(2,1)}, bf16[576,768]{1,0:T(8,128)(2,1)S(1)}, u32[]{:S(2)}, u32[]{:S(2)}) collective-permute-start(bf16[576,768]{1,0:T(8,128)(2,1)} %bitcast.19), channel_id=1, source_target_pairs={{0,1},{1,0},{2,3},{3,2},{4,5},{5,4},{6,7},{7,6},{8,9},{9,8},{10,11... | collective-permute-start | bytes 2654216 | tf_op jit(solution)/shard_map/ppermute | solution.py:271
  19.6 10.2 %copy-start = (bf16[8,512,128]{2,1,0:T(8,128)(2,1)S(1)}, bf16[8,512,128]{2,1,0:T(8,128)(2,1)}, u32[]{:S(2)}) copy-start(bf16[8,512,128]{2,1,0:T(8,128)(2,1)} %param.15) | copy-start | bytes 3145732
  19.6 53.1 %copy-start.3 = (bf16[1,128,3584]{2,1,0:T(8,128)(2,1)S(1)}, bf16[1,128,3584]{2,1,0:T(8,128)(2,1)}, u32[]{:S(2)}) copy-start(bf16[1,128,3584]{2,1,0:T(8,128)(2,1)} %param.21) | copy-start | bytes 2752516
  29.8 43.0 %copy-start.2 = (bf16[1,3584,128]{2,1,0:T(8,128)(2,1)S(1)}, bf16[1,3584,128]{2,1,0:T(8,128)(2,1)}, u32[]{:S(2)}) copy-start(bf16[1,3584,128]{2,1,0:T(8,128)(2,1)} %param.20) | copy-start | bytes 2752516
  30.2 42.5 %copy-start.1 = (bf16[1,3584,128]{2,1,0:T(8,128)(2,1)S(1)}, bf16[1,3584,128]{2,1,0:T(8,128)(2,1)}, u32[]{:S(2)}) copy-start(bf16[1,3584,128]{2,1,0:T(8,128)(2,1)} %param.19) | copy-start | bytes 2752516

commit v9 on v7

--- a/solution.py
+++ b/solution.py
@@ -228,18 +228,12 @@
     share = share + jnp.where(lax.axis_index("head") == 0, mixed_ref[...], 0.0)
     groups, rows = out_ref.shape[0], share.shape[0]
     for i, owner in enumerate(ring("head", groups)):
-        group = owner * rows // groups // 8
-        out_ref[i] = share[group * 8 : group * 8 + 8]
+        out_ref[i] = share[owner * rows // groups : (owner + 1) * rows // groups]
 
 
 def finish_body(parts_ref, out_ref):
-    share = jnp.sum(parts_ref[...], axis=0)
-    rows, columns = out_ref.shape
-    place = lax.axis_index("head") % (8 // rows)
-    mine = share[:rows]
-    for i in range(1, 8 // rows):
-        mine = jnp.where(place == i, share[i * rows : (i + 1) * rows], mine)
-    out_ref[...] = mine[:, :columns].astype(bf16)
+    columns = out_ref.shape[1]
+    out_ref[...] = jnp.sum(parts_ref[...], axis=0)[:, :columns].astype(bf16)
 
 
 def local(
@@ -353,7 +347,7 @@
         weight,
     )
     outcome = exchange(outcome, "expert")
-    moe = call(gather_body, shape((head_n, 8, LANES), f32), [VM] * 3, outcome, combine, mixed)
+    moe = call(gather_body, shape((head_n, row_share, LANES), f32), [VM] * 3, outcome, combine, mixed)
     return call(finish_body, shape((row_share, columns), bf16), [VM], exchange(moe, "head"))
 
 

time: 99.6 us -> 99.1 us (level)
  no operation moved by 1% of the time
where the time goes in v9:
time: 99.1 us; the launch traced here: 98.6 us
  blocking collectives  85 us (86%)
  starting transfers between devices  8.77 us (9%)
  Pallas kernels  4.82 us (5%)
    all_to_all x7, blocking collectives, exchange(): lax.all_to_all(blocks, axis, split_axis=0, concat_axis=0, tiled=True, axi...  85 us
    ppermute x1, starting transfers between devices, local(): lax.ppermute(kv_cache[0].T, 'head', [(i, i ^ 1) for i in range(head_n)])  8.77 us
    pallas_call x7, Pallas kernels, call(): pl.pallas_call(body, out_shape=out_shape, in_specs=in_specs, out_specs=ja...  3.36 us
  transfers between devices with their start and end apart: 1, of which 0 were waited for; matrix products, arithmetic and copies ran while one was open for 0% of the time, Pallas kernels for 1%

profile of v9, /device:TPU:1, one launch (start us, length us, event | category | flops | bytes accessed | tf_op | source)
XLA Modules:
  0.0 98.6 jit_solution(13968214688870199535)
XLA Ops:
  0.0 8.8 %collective-permute-start = (bf16[576,768]{1,0:T(8,128)(2,1)}, bf16[576,768]{1,0:T(8,128)(2,1)S(1)}, u32[]{:S(2)}, u32[]{:S(2)}) collective-permute-start(bf16[576,768]{1,0:T(8,128)(2,1)} %bitcast.19), channel_id=1, source_target_pairs={{0,1},{1,0},{2,3},{3,2},{4,5},{5,4},{6,7},{7,6},{8,9},{9,8},{10,11... | collective-permute-start | bytes 2654216 | tf_op jit(solution)/shard_map/ppermute | solution.py:265
  8.8 1.5 %shard_map.118 = (bf16[8,8,576]{2,1,0:T(8,128)(2,1)S(1)}, bf16[512,32]{1,0:T(8,128)(2,1)S(1)}, bf16[32,512]{1,0:T(8,128)(2,1)S(1)}, f32[16,128]{1,0:T(8,128)S(1)...) custom-call(bf16[1,8,576]{2,1,0:T(8,128)(2,1)} %queries_any.1, ...), custom_call_target="tpu_custom_call" | custom-call | tf_op jit(solution)/shard_map/pallas_call | solution.py:266
  10.3 9.4 %all_to_all.35 = bf16[8,8,576]{2,1,0:T(8,128)(2,1)S(1)} all-to-all(bf16[8,8,576]{2,1,0:T(8,128)(2,1)S(1)} %get-tuple-element.17), channel_id=1, replica_groups={{10,12,14,0,2,4,6,8},{11,13,15,1,3,5,7,9},{26,28,30,16,18,20,22,24},{27..., dimensions={0} | all-to-all | bytes 147456 | tf_op jit(solution)/shard_map/all_to_all | solution.py:44
  19.6 0.0 collective-permute-done.other_ref
  19.6 0.0 copy-start
  19.6 0.0 copy-start.3
  19.6 1.1 %shard_map.119 = bf16[64,640]{1,0:T(8,128)(2,1)S(1)} custom-call(f32[8,1536]{1,0:T(8,128)S(1)} %get-tuple-element.16.chosen_ref, bf16[64,576]{1,0:T(8,128)(2,1)S(1)} %bitcast.17, bf16[576,768]{1,0:T(8,128)(2,1)S(1)} %get-tuple-element.18.mine_ref, bf16[576,768]{1,0:T(8,128)(2,1)S(1)} %collective-permute-done.other_ref), custom_call_target="tpu_custom_call" | custom-call | tf_op jit(solution)/shard_map/pallas_call | solution.py:28
  20.7 9.1 %all_to_all.36.parts_ref = bf16[8,8,640]{2,1,0:T(8,128)(2,1)S(1)} all-to-all(bf16[8,8,640]{2,1,0:T(8,128)(2,1)S(1)} %bitcast.18), channel_id=1, replica_groups={{10,12,14,0,2,4,6,8},{11,13,15,1,3,5,7,9},{26,28,30,16,18,20,22,24},{27..., dimensions={0} | all-to-all | bytes 163840 | tf_op jit(solution)/shard_map/all_to_all | solution.py:44
  29.8 0.0 copy-done
  29.8 0.0 copy-start.2
  29.8 0.4 shard_map.120
  30.2 0.0 copy-start.1
  30.3 14.7 %all_to_all.37.vals_ref = bf16[32,8,128]{2,1,0:T(8,128)(2,1)S(1)} all-to-all(bf16[32,8,128]{2,1,0:T(8,128)(2,1)S(1)} %shard_map.120), channel_id=1, replica_groups={{352,368,384,400,416,432,448,464,480,496,0,16,32,48,64,80,96,112,128,14..., dimensions={0} | all-to-all | bytes 131072 | tf_op jit(solution)/shard_map/all_to_all | solution.py:44
  44.9 0.2 shard_map.121
  45.1 14.5 %all_to_all.38.parts_ref = bf16[16,32,128]{2,1,0:T(8,128)(2,1)S(1)} all-to-all(bf16[16,32,128]{2,1,0:T(8,128)(2,1)S(1)} %shard_map.121), channel_id=1, replica_groups={{11,12,13,14,15,0,1,2,3,4,5,6,7,8,9,10},{27,28,29,30,31,16,17,18,19,20,..., dimensions={0} | all-to-all | bytes 262144 | tf_op jit(solution)/shard_map/all_to_all | solution.py:44
  59.6 0.3 shard_map.122
  59.9 12.9 %all_to_all.39.slots_ref = bf16[32,16,128]{2,1,0:T(8,128)(2,1)S(1)} all-to-all(bf16[32,16,128]{2,1,0:T(8,128)(2,1)S(1)} %get-tuple-element.23), channel_id=1, replica_groups={{352,368,384,400,416,432,448,464,480,496,0,16,32,48,64,80,96,112,128,14..., dimensions={0} | all-to-all | bytes 262144 | tf_op jit(solution)/shard_map/all_to_all | solution.py:44
  72.8 0.0 copy-done.3
  72.8 0.0 copy-done.2
  72.8 0.0 copy-done.1
  72.8 0.7 shard_map.123
  73.5 13.2 %all_to_all.40.parts_ref = bf16[32,16,128]{2,1,0:T(8,128)(2,1)S(1)} all-to-all(bf16[32,16,128]{2,1,0:T(8,128)(2,1)S(1)} %shard_map.123), channel_id=1, replica_groups={{352,368,384,400,416,432,448,464,480,496,0,16,32,48,64,80,96,112,128,14..., dimensions={0} | all-to-all | bytes 262144 | tf_op jit(solution)/shard_map/all_to_all | solution.py:44
  86.7 0.1 shard_map.124
  86.8 11.3 %all_to_all.41.parts_ref = f32[16,2,128]{2,1,0:T(2,128)S(1)} all-to-all(f32[16,2,128]{2,1,0:T(2,128)S(1)} %shard_map.124), channel_id=1, replica_groups={{11,12,13,14,15,0,1,2,3,4,5,6,7,8,9,10},{27,28,29,30,31,16,17,18,19,20,..., dimensions={0} | all-to-all | bytes 32768 | tf_op jit(solution)/shard_map/all_to_all | solution.py:44
  98.1 0.5 shard_map.125
Async XLA Ops:
  0.0 19.6 %collective-permute-start = (bf16[576,768]{1,0:T(8,128)(2,1)}, bf16[576,768]{1,0:T(8,128)(2,1)S(1)}, u32[]{:S(2)}, u32[]{:S(2)}) collective-permute-start(bf16[576,768]{1,0:T(8,128)(2,1)} %bitcast.19), channel_id=1, source_target_pairs={{0,1},{1,0},{2,3},{3,2},{4,5},{5,4},{6,7},{7,6},{8,9},{9,8},{10,11... | collective-permute-start | bytes 2654216 | tf_op jit(solution)/shard_map/ppermute | solution.py:265
  19.6 10.1 %copy-start = (bf16[8,512,128]{2,1,0:T(8,128)(2,1)S(1)}, bf16[8,512,128]{2,1,0:T(8,128)(2,1)}, u32[]{:S(2)}) copy-start(bf16[8,512,128]{2,1,0:T(8,128)(2,1)} %param.15) | copy-start | bytes 3145732
  19.6 53.1 %copy-start.3 = (bf16[1,128,3584]{2,1,0:T(8,128)(2,1)S(1)}, bf16[1,128,3584]{2,1,0:T(8,128)(2,1)}, u32[]{:S(2)}) copy-start(bf16[1,128,3584]{2,1,0:T(8,128)(2,1)} %param.21) | copy-start | bytes 2752516
  29.8 43.0 %copy-start.2 = (bf16[1,3584,128]{2,1,0:T(8,128)(2,1)S(1)}, bf16[1,3584,128]{2,1,0:T(8,128)(2,1)}, u32[]{:S(2)}) copy-start(bf16[1,3584,128]{2,1,0:T(8,128)(2,1)} %param.20) | copy-start | bytes 2752516
  30.2 42.5 %copy-start.1 = (bf16[1,3584,128]{2,1,0:T(8,128)(2,1)S(1)}, bf16[1,3584,128]{2,1,0:T(8,128)(2,1)}, u32[]{:S(2)}) copy-start(bf16[1,3584,128]{2,1,0:T(8,128)(2,1)} %param.19) | copy-start | bytes 2752516
